TPU v7x, 32 devices: a whole 2x2x4 slice. The times are simulated.
32 devices in a mesh: section: 2 (over core), dp: 4 (over z), ctx: 4 (over y, x).
Axes of the slice: x: 2, y: 2, z: 4, core: 2. Of those that a mesh axis runs over, the one named last changes fastest.
Arguments:
- ends_in: bfloat16 [2, 6, 2048, 768], P('section', None, ('dp', 'ctx')), may hold values from -6 to 6
- begins: int32 [6, 32], P(None, ('dp', 'ctx')), may hold values from 0 to 1, as said below
- filled: int32 [6, 32], P(None, ('dp', 'ctx')), may hold values from 1 to 64, as said below
- first_gain: bfloat16 [2, 768], P('section'), may hold values from 0.5 to 1.5
- first_shift: bfloat16 [2, 768], P('section'), may hold values from -4 to 4
- qkv_weight: bfloat16 [2, 768, 2304], P('section'), may hold values from -0.21875 to 0.21875
- qkv_bias: bfloat16 [2, 2304], P('section'), may hold values from -4 to 4
- query_map: bfloat16 [2, 64, 768], P('section'), may hold values from -1.5 to 1.5
- key_map: bfloat16 [2, 64, 768], P('section'), may hold values from -1.5 to 1.5
- out_weight: bfloat16 [2, 768, 768], P('section'), may hold values from -3.5 to 3.5
- out_bias: bfloat16 [2, 768], P('section'), may hold values from -4 to 4
- second_gain: bfloat16 [2, 768], P('section'), may hold values from 0.5 to 1.5
- second_shift: bfloat16 [2, 768], P('section'), may hold values from -4 to 4
- up_weight: bfloat16 [2, 768, 3072], P('section'), may hold values from -0.21875 to 0.21875
- up_bias: bfloat16 [2, 3072], P('section'), may hold values from -4 to 4
- down_weight: bfloat16 [2, 3072, 768], P('section'), may hold values from -0.109375 to 0.109375
- down_bias: bfloat16 [2, 768], P('section'), may hold values from -4 to 4
Outputs:
- ends_out: bfloat16 [2, 6, 2048, 768], P('section', None, ('dp', 'ctx'))
- grad_first_gain: float32 [2, 768], P('section')
- grad_first_shift: float32 [2, 768], P('section')
- grad_qkv_weight: float32 [2, 768, 2304], P('section')
- grad_qkv_bias: float32 [2, 2304], P('section')
- grad_query_map: float32 [2, 64, 768], P('section')
- grad_key_map: float32 [2, 64, 768], P('section')
- grad_out_weight: float32 [2, 768, 768], P('section')
- grad_out_bias: float32 [2, 768], P('section')
- grad_second_gain: float32 [2, 768], P('section')
- grad_second_shift: float32 [2, 768], P('section')
- grad_up_weight: float32 [2, 768, 3072], P('section')
- grad_up_bias: float32 [2, 3072], P('section')
- grad_down_weight: float32 [2, 3072, 768], P('section')
- grad_down_bias: float32 [2, 768], P('section')
Inputs may be any that keep to these rules, and one draw needn't show every extreme that they name: Each group of 8 blocks (one index of dp) has begins = 1 at its first block. In one micro-batch of each group, drawn from the seed, that is its only start; elsewhere sequences cover 2 to 31 blocks, heavy tailed, the last one cut at the group's end. `filled`: 64 except in the last block of a sequence; valid tokens come first in a block.
All inputs are finite; a program needn't handle non-finite values.
Results may differ from a plain program's by a relative error of at most 0.012.
The roundings to bfloat16 on the way count: a program that leaves them out, or rounds other values in their place, can miss the bound.
Values may be sent and summed in bfloat16 or wider, within the bound.
A program may use at most 448 MiB of HBM per device.

v0:
```python
import jax
import jax.numpy as jnp
from jax import lax
from jax.sharding import PartitionSpec as P

BLOCK = 64


epsilon = 1e-05
highest = lax.Precision.HIGHEST


def prefix(shard, axis, combine, identity, reverse):
    size, mine = (lax.axis_size(axis), lax.axis_index(axis))
    everything = jax.tree.map(lambda part: lax.all_gather(part, axis), shard)
    start = jax.tree.map(
        lambda part, zero: jnp.broadcast_to(jnp.asarray(zero, part.dtype), part.shape),
        shard,
        identity,
    )

    def step(k, before):
        at = size - 1 - k if reverse else k
        reached = at > mine if reverse else at < mine
        new = combine(before, jax.tree.map(lambda part: part[at], everything))
        return jax.tree.map(lambda a, b: jnp.where(reached, a, b), new, before)

    return lax.fori_loop(0, size, step, start)


def passed_along(shard, axis, by):
    size = lax.axis_size(axis)
    pairs = [(i, i + by) for i in range(size) if 0 <= i + by < size]
    return lax.ppermute(shard, axis, pairs)


def matmul(left, right):
    return jnp.dot(left, right, preferred_element_type=jnp.float32)


def times_transposed(left, right):
    return lax.dot_general(
        left, right, (((1,), (1,)), ((), ())), preferred_element_type=jnp.float32
    )


def outer_sum(left, right):
    return lax.dot_general(
        left, right, (((0,), (0,)), ((), ())), preferred_element_type=jnp.float32
    )


def layer_norm(rows, gain, shift):
    average = jnp.mean(rows, -1, keepdims=True)
    centred = rows - average
    variance = jnp.mean(centred * centred, -1, keepdims=True)
    return centred * lax.rsqrt(variance + epsilon) * gain + shift


def feature_map(logits):
    return jnp.concatenate([jax.nn.softmax(logits, -1), jax.nn.softmax(-logits, -1)], -1)


def gelu_tanh(values):
    return jax.nn.gelu(values, approximate=True)


def combine_states(earlier, later):
    kept_share = 1.0 - later[2]
    return (
        later[0] + kept_share * earlier[0],
        later[1] + kept_share * earlier[1],
        jnp.maximum(earlier[2], later[2]),
    )


def empty_like(states):
    return jax.tree.map(jnp.zeros_like, states)


def carry_forward(local):
    return prefix(local, "ctx", combine_states, empty_like(local), False)


def carry_back(local):
    return prefix(local, "ctx", combine_states, empty_like(local), True)


def block_layout(begin_row, filled_row):
    starting = begin_row.astype(jnp.float32)
    counted = jnp.cumsum(starting)
    token_segment = jnp.repeat(counted, BLOCK)
    usable = (jnp.arange(BLOCK)[None, :] < filled_row[:, None]).astype(jnp.float32).reshape(-1)
    before = (token_segment == 0.0).astype(jnp.float32)
    trailing = (token_segment == counted[-1]).astype(jnp.float32) * usable
    positions = jnp.arange(token_segment.shape[0])
    allowed = (
        (token_segment[:, None] == token_segment[None, :])
        & (positions[None, :] <= positions[:, None])
    ).astype(jnp.float32)
    restart = jnp.max(starting)
    return (before, trailing, usable, allowed, restart)


def split_heads(projected, head_size):
    token_count = projected.shape[0]
    head_count = projected.shape[1] // (3 * head_size)
    return projected.reshape(token_count, 3, head_count, head_size)


def front_half(rows, weights):
    normed = layer_norm(
        rows, weights[0].astype(jnp.float32), weights[1].astype(jnp.float32)
    ).astype(jnp.bfloat16)
    projected = (matmul(normed, weights[2]) + weights[3].astype(jnp.float32)).astype(jnp.bfloat16)
    head_size = weights[4].shape[0]
    split = split_heads(projected, head_size)
    head_count = split.shape[2]
    query_logits = jnp.einsum(
        "thi,ihj->thj",
        split[:, 0],
        weights[4].reshape(head_size, head_count, head_size),
        preferred_element_type=jnp.float32,
    )
    key_logits = jnp.einsum(
        "thi,ihj->thj",
        split[:, 1],
        weights[5].reshape(head_size, head_count, head_size),
        preferred_element_type=jnp.float32,
    )
    query_phi = feature_map(query_logits).astype(jnp.bfloat16)
    key_phi = feature_map(key_logits).astype(jnp.bfloat16)
    return (normed, projected, query_logits, key_logits, query_phi, key_phi)


def local_state(key_phi, projected, geometry):
    values_h = split_heads(projected, key_phi.shape[2] // 2)[:, 2]
    weighted = key_phi * geometry[1][:, None, None].astype(jnp.bfloat16)
    states = jnp.einsum("shf,shd->hfd", weighted, values_h, preferred_element_type=jnp.float32)
    key_sums = jnp.sum(weighted.astype(jnp.float32), 0)
    return (states, key_sums, geometry[4])


def back_half(rows, weights, geometry, front, carried):
    normed, projected, query_logits, key_logits, query_phi, key_phi = front
    before, trailing, usable, allowed, restart = geometry
    values_h = split_heads(projected, key_phi.shape[2] // 2)[:, 2]
    key_rows = key_phi * usable[:, None, None].astype(jnp.bfloat16)
    scores = (
        jnp.einsum("thf,shf->hts", query_phi, key_rows, preferred_element_type=jnp.float32)
        * allowed[None]
    )
    value_wide = values_h.astype(jnp.float32)
    query_wide = query_phi.astype(jnp.float32)
    numerator = jnp.einsum("hts,shd->thd", scores, value_wide, precision=highest)
    numerator = numerator + before[:, None, None] * jnp.einsum(
        "thf,hfd->thd", query_wide, carried[0], precision=highest
    )
    denominator = jnp.einsum("hts->th", scores) + before[:, None] * jnp.einsum(
        "thf,hf->th", query_wide, carried[1], precision=highest
    )
    attended = (numerator / denominator[..., None]).reshape(rows.shape[0], -1).astype(jnp.bfloat16)
    residual = rows + matmul(attended, weights[6]) + weights[7].astype(jnp.float32)
    normed_two = layer_norm(
        residual, weights[8].astype(jnp.float32), weights[9].astype(jnp.float32)
    ).astype(jnp.bfloat16)
    hidden = matmul(normed_two, weights[10]) + weights[11].astype(jnp.float32)
    activated = gelu_tanh(hidden).astype(jnp.bfloat16)
    output = residual + matmul(activated, weights[12]) + weights[13].astype(jnp.float32)
    saved = (
        attended,
        residual,
        normed_two,
        hidden,
        activated,
        key_rows,
        scores,
        numerator,
        denominator,
        values_h,
    )
    return (output, saved)


def block_backward(rows, weights, geometry, carried, grad_out):
    front = front_half(rows, weights)
    normed, projected, query_logits, key_logits, query_phi, key_phi = front
    output, saved = back_half(rows, weights, geometry, front, carried)
    (
        attended,
        residual,
        normed_two,
        hidden,
        activated,
        key_rows,
        scores,
        numerator,
        denominator,
        values_h,
    ) = saved
    before, trailing, usable, allowed, restart = geometry
    grad_down = grad_out.astype(jnp.bfloat16)
    down_w_grad = outer_sum(activated, grad_down)
    down_b_grad = jnp.sum(grad_down.astype(jnp.float32), 0)
    grad_active = times_transposed(grad_down, weights[12])
    grad_hidden = jax.vjp(gelu_tanh, hidden)[1](grad_active)[0].astype(jnp.bfloat16)
    up_w_grad = outer_sum(normed_two, grad_hidden)
    up_b_grad = jnp.sum(grad_hidden.astype(jnp.float32), 0)
    grad_normed_two = times_transposed(grad_hidden, weights[10])
    second_back = jax.vjp(
        layer_norm, residual, weights[8].astype(jnp.float32), weights[9].astype(jnp.float32)
    )[1](grad_normed_two)
    grad_residual = grad_out + second_back[0]
    grad_branch = grad_residual.astype(jnp.bfloat16)
    out_w_grad = outer_sum(attended, grad_branch)
    out_b_grad = jnp.sum(grad_branch.astype(jnp.float32), 0)
    head_size = weights[4].shape[0]
    grad_attended = times_transposed(grad_branch, weights[6]).reshape(rows.shape[0], -1, head_size)
    attended_wide = numerator / denominator[..., None]
    grad_numer = grad_attended / denominator[..., None]
    grad_denom = -jnp.sum(grad_attended * attended_wide, -1) / denominator
    query_wide = query_phi.astype(jnp.float32)
    key_wide = key_rows.astype(jnp.float32)
    value_wide = values_h.astype(jnp.float32)
    query_before = query_wide * before[:, None, None]
    local_grads = (
        jnp.einsum("thf,thd->hfd", query_before, grad_numer, precision=highest),
        jnp.einsum("thf,th->hf", query_before, grad_denom, precision=highest),
        restart,
    )
    grad_carried = carry_back(local_grads)
    grad_scores = (
        jnp.einsum("thd,shd->hts", grad_numer, value_wide, precision=highest)
        + grad_denom.T[:, :, None]
    ) * allowed[None]
    weighted = key_phi.astype(jnp.float32) * trailing[:, None, None]
    grad_query_phi = jnp.einsum("hts,shf->thf", grad_scores, key_wide, precision=highest)
    grad_query_phi = grad_query_phi + before[:, None, None] * (
        jnp.einsum("thd,hfd->thf", grad_numer, carried[0], precision=highest)
        + grad_denom[:, :, None] * carried[1][None]
    )
    grad_key_phi = (
        jnp.einsum("hts,thf->shf", grad_scores, query_wide, precision=highest)
        * usable[:, None, None]
    )
    grad_key_phi = grad_key_phi + trailing[:, None, None] * (
        jnp.einsum("shd,hfd->shf", value_wide, grad_carried[0], precision=highest)
        + grad_carried[1][None]
    )
    grad_values = jnp.einsum("hts,thd->shd", scores, grad_numer, precision=highest) + jnp.einsum(
        "shf,hfd->shd", weighted, grad_carried[0], precision=highest
    )
    grad_query_logits = jax.vjp(feature_map, query_logits)[1](grad_query_phi)[0].astype(
        jnp.bfloat16
    )
    grad_key_logits = jax.vjp(feature_map, key_logits)[1](grad_key_phi)[0].astype(jnp.bfloat16)
    split = split_heads(projected, head_size)
    head_count = split.shape[2]
    query_table = weights[4].reshape(head_size, head_count, head_size)
    key_table = weights[5].reshape(head_size, head_count, head_size)
    grad_queries = jnp.einsum(
        "thj,ihj->thi", grad_query_logits, query_table, preferred_element_type=jnp.float32
    )
    grad_keys = jnp.einsum(
        "thj,ihj->thi", grad_key_logits, key_table, preferred_element_type=jnp.float32
    )
    query_map_grad = jnp.einsum(
        "thi,thj->ihj", split[:, 0], grad_query_logits, preferred_element_type=jnp.float32
    ).reshape(head_size, -1)
    key_map_grad = jnp.einsum(
        "thi,thj->ihj", split[:, 1], grad_key_logits, preferred_element_type=jnp.float32
    ).reshape(head_size, -1)
    grad_projected = (
        jnp.stack([grad_queries, grad_keys, grad_values], 1)
        .reshape(rows.shape[0], -1)
        .astype(jnp.bfloat16)
    )
    qkv_w_grad = outer_sum(normed, grad_projected)
    qkv_b_grad = jnp.sum(grad_projected.astype(jnp.float32), 0)
    grad_normed = times_transposed(grad_projected, weights[2])
    first_back = jax.vjp(
        layer_norm, rows, weights[0].astype(jnp.float32), weights[1].astype(jnp.float32)
    )[1](grad_normed)
    grad_rows = grad_residual + first_back[0]
    grads = (
        first_back[1],
        first_back[2],
        qkv_w_grad,
        qkv_b_grad,
        query_map_grad,
        key_map_grad,
        out_w_grad,
        out_b_grad,
        second_back[1],
        second_back[2],
        up_w_grad,
        up_b_grad,
        down_w_grad,
        down_b_grad,
    )
    return (grad_rows, grads)


def select_section(first_section, early, late):
    return jax.tree.map(
        lambda early_leaf, late_leaf: jnp.where(first_section, early_leaf, late_leaf), early, late
    )


def body(
    ends_in,
    begins,
    filled,
    first_gain,
    first_shift,
    qkv_weight,
    qkv_bias,
    query_map,
    key_map,
    out_weight,
    out_bias,
    second_gain,
    second_shift,
    up_weight,
    up_bias,
    down_weight,
    down_bias,
):
    weights = tuple(
        (
            weight[0]
            for weight in (
                first_gain,
                first_shift,
                qkv_weight,
                qkv_bias,
                query_map,
                key_map,
                out_weight,
                out_bias,
                second_gain,
                second_shift,
                up_weight,
                up_bias,
                down_weight,
                down_bias,
            )
        )
    )
    first_section = lax.axis_index("section") == 0
    local_rows = ends_in[0]
    micro_count = local_rows.shape[0]
    layouts = [
        block_layout(begins[micro_index], filled[micro_index]) for micro_index in range(micro_count)
    ]
    received = jnp.zeros_like(local_rows[0])
    kept_rows, kept_states, produced = ([], [], [])
    for position in range(micro_count + 1):
        geometry = select_section(
            first_section, layouts[min(position, micro_count - 1)], layouts[max(position - 1, 0)]
        )
        current = jnp.where(first_section, local_rows[min(position, micro_count - 1)], received)
        rows = current.astype(jnp.float32)
        front = front_half(rows, weights)
        carried = carry_forward(local_state(front[5], front[1], geometry))
        output = back_half(rows, weights, geometry, front, carried)[0].astype(jnp.bfloat16)
        kept_rows.append(current)
        kept_states.append(carried)
        produced.append(output)
        if position < micro_count:
            received = passed_along(output, "section", 1)
    incoming = jnp.zeros(local_rows.shape[1:], jnp.float32)
    totals = None
    back_rows = []
    for position in range(micro_count + 1):
        early = max(position - 1, 0)
        late = min(position + 1, micro_count)
        rows = select_section(first_section, kept_rows[early], kept_rows[late]).astype(jnp.float32)
        carried = select_section(first_section, kept_states[early], kept_states[late])
        geometry = select_section(
            first_section,
            layouts[min(early, micro_count - 1)],
            layouts[min(position, micro_count - 1)],
        )
        own_grad = local_rows[min(position, micro_count - 1)].astype(jnp.float32) * float(
            position < micro_count
        )
        grad_out = jnp.where(first_section, incoming, own_grad)
        grad_rows, grads = block_backward(rows, weights, geometry, carried, grad_out)
        back_rows.append(grad_rows.astype(jnp.bfloat16))
        totals = grads if totals is None else jax.tree.map(jnp.add, totals, grads)
        if position < micro_count:
            incoming = passed_along(back_rows[-1], "section", -1).astype(jnp.float32)
    totals = lax.psum(totals, ("dp", "ctx"))
    ends_out = jnp.where(first_section, jnp.stack(back_rows[1:]), jnp.stack(produced[1:]))[None]
    return (ends_out,) + tuple((total[None] for total in totals))


def solution(mesh):
    placed = (
        P("section", None, ("dp", "ctx"), None),
        P(None, ("dp", "ctx")),
        P(None, ("dp", "ctx")),
        P("section", None),
        P("section", None),
        P("section", None, None),
        P("section", None),
        P("section", None, None),
        P("section", None, None),
        P("section", None, None),
        P("section", None),
        P("section", None),
        P("section", None),
        P("section", None, None),
        P("section", None),
        P("section", None, None),
        P("section", None),
    )
    return jax.shard_map(
        body,
        mesh=mesh,
        in_specs=placed,
        out_specs=(
            P("section", None, ("dp", "ctx"), None),
            P("section", None),
            P("section", None),
            P("section", None, None),
            P("section", None),
            P("section", None, None),
            P("section", None, None),
            P("section", None, None),
            P("section", None),
            P("section", None),
            P("section", None),
            P("section", None, None),
            P("section", None),
            P("section", None, None),
            P("section", None),
        ),
        check_vma=False,
    )
```

profile of v0, /device:TPU:0, one launch (start us, length us, event | category | flops | bytes accessed | tf_op | source)
XLA Modules:
  0.0 2657.5 jit_solution(3142170512397894475)
XLA Ops:
  95.1 11.1 all-gather.28
  139.6 9.8 all-reduce.14
  167.5 37.7 %while.238 = (s32[]{:T(128)}, f32[12,128,64]{2,1,0:T(8,128)}, f32[12,128]{1,0:T(8,128)}, s32[]{:T(128)}, f32[4,12,128,64]{2,3,1,0:T(8,128)}, /*index=5*/f32[4]{0...) while((s32[]{:T(128)}, f32[12,128,64]{2,1,0:T(8,128)}, f32[12,128]{1,0:T(8,128)}, ...), condition=%wide.region_14.15_spmd.clone, body=%wide.region_13.14_spmd.clone.sunk | while | flops 399365 | bytes 2771115 | solution.py:28
  297.9 37.8 %while.239 = (s32[]{:T(128)}, f32[12,128,64]{2,1,0:T(8,128)}, f32[12,128]{1,0:T(8,128)}, s32[]{:T(128)}, f32[4,12,128,64]{2,3,1,0:T(8,128)}, /*index=5*/f32[4]{0...) while((s32[]{:T(128)}, f32[12,128,64]{2,1,0:T(8,128)}, f32[12,128]{1,0:T(8,128)}, ...), condition=%wide.region_38.39_spmd.clone, body=%wide.region_37.38_spmd.clone.sunk | while | flops 399365 | bytes 2771115 | solution.py:28
  367.4 13.5 collective-permute-start.2
  392.8 8.7 all-gather.30
  420.8 37.7 %while.240 = (s32[]{:T(128)}, f32[12,128,64]{2,1,0:T(8,128)}, f32[12,128]{1,0:T(8,128)}, s32[]{:T(128)}, f32[4,12,128,64]{2,3,1,0:T(8,128)}, /*index=5*/f32[4]{0...) while((s32[]{:T(128)}, f32[12,128,64]{2,1,0:T(8,128)}, ...), condition=%wide.region_48.49_spmd.clone, body=%wide.region_47.48_spmd.clone.sunk | while | flops 399369 | bytes 2771177 | solution.py:28
  552.5 37.5 %while.241 = (s32[]{:T(128)}, f32[12,128,64]{2,1,0:T(8,128)}, f32[12,128]{1,0:T(8,128)}, s32[]{:T(128)}, f32[4,12,128,64]{2,3,1,0:T(8,128)}, /*index=5*/f32[4]{0...) while((s32[]{:T(128)}, f32[12,128,64]{2,1,0:T(8,128)}, f32[12,128]{1,0:T(8,128)}, ...), condition=%wide.region_80.81_spmd.clone, body=%wide.region_79.80_spmd.clone.sunk | while | flops 399365 | bytes 2771115 | solution.py:28
  636.1 8.9 all-gather.32
  664.2 37.5 %while.242 = (s32[]{:T(128)}, f32[12,128,64]{2,1,0:T(8,128)}, f32[12,128]{1,0:T(8,128)}, s32[]{:T(128)}, f32[4,12,128,64]{2,3,1,0:T(8,128)}, /*index=5*/f32[4]{0...) while((s32[]{:T(128)}, f32[12,128,64]{2,1,0:T(8,128)}, ...), condition=%wide.region_90.91_spmd.clone, body=%wide.region_89.90_spmd.clone.sunk | while | flops 399369 | bytes 2771177 | solution.py:28
  756.8 8.7 all-gather.33
  796.7 38.0 %while.243 = (s32[]{:T(128)}, f32[12,128,64]{2,1,0:T(8,128)}, f32[12,128]{1,0:T(8,128)}, s32[]{:T(128)}, f32[4,12,128,64]{2,3,1,0:T(8,128)}, /*index=5*/f32[4]{0...) while((s32[]{:T(128)}, f32[12,128,64]{2,1,0:T(8,128)}, ...), condition=%wide.region_122.123_spmd.clone, body=%wide.region_121.122_spmd.clone.sunk | while | flops 399365 | bytes 2771115 | solution.py:28
  880.7 8.9 all-gather.34
  908.7 37.8 %while.244 = (s32[]{:T(128)}, f32[12,128,64]{2,1,0:T(8,128)}, f32[12,128]{1,0:T(8,128)}, s32[]{:T(128)}, f32[4,12,128,64]{2,3,1,0:T(8,128)}, /*index=5*/f32[4]{0...) while((s32[]{:T(128)}, f32[12,128,64]{2,1,0:T(8,128)}, ...), condition=%wide.region_132.133_spmd.clone, body=%wide.region_131.132_spmd.clone.sunk | while | flops 399369 | bytes 2771177 | solution.py:28
  1041.5 37.7 %while.245 = (s32[]{:T(128)}, f32[12,128,64]{2,1,0:T(8,128)}, f32[12,128]{1,0:T(8,128)}, s32[]{:T(128)}, f32[4,12,128,64]{2,3,1,0:T(8,128)}, /*index=5*/f32[4]{0...) while((s32[]{:T(128)}, f32[12,128,64]{2,1,0:T(8,128)}, ...), condition=%wide.region_164.165_spmd.clone, body=%wide.region_163.164_spmd.clone.sunk | while | flops 399365 | bytes 2771115 | solution.py:28
  1125.3 8.9 all-gather.36
  1153.4 37.9 %while.246 = (s32[]{:T(128)}, f32[12,128,64]{2,1,0:T(8,128)}, f32[12,128]{1,0:T(8,128)}, s32[]{:T(128)}, f32[4,12,128,64]{2,3,1,0:T(8,128)}, /*index=5*/f32[4]{0...) while((s32[]{:T(128)}, f32[12,128,64]{2,1,0:T(8,128)}, ...), condition=%wide.region_174.175_spmd.clone, body=%wide.region_173.174_spmd.clone.sunk | while | flops 399369 | bytes 2771177 | solution.py:28
  1246.4 8.7 all-gather.37
  1286.3 37.6 %while.247 = (s32[]{:T(128)}, f32[12,128,64]{2,1,0:T(8,128)}, f32[12,128]{1,0:T(8,128)}, s32[]{:T(128)}, f32[4,12,128,64]{2,3,1,0:T(8,128)}, /*index=5*/f32[4]{0...) while((s32[]{:T(128)}, f32[12,128,64]{2,1,0:T(8,128)}, ...), condition=%wide.region_206.207_spmd.clone, body=%wide.region_205.206_spmd.clone.sunk | while | flops 399365 | bytes 2771115 | solution.py:28
  1369.9 8.9 all-gather.38
  1397.9 37.9 %while.248 = (s32[]{:T(128)}, f32[12,128,64]{2,1,0:T(8,128)}, f32[12,128]{1,0:T(8,128)}, s32[]{:T(128)}, f32[4,12,128,64]{2,3,1,0:T(8,128)}, /*index=5*/f32[4]{0...) while((s32[]{:T(128)}, f32[12,128,64]{2,1,0:T(8,128)}, ...), condition=%wide.region_216.217_spmd.clone, body=%wide.region_215.216_spmd.clone.sunk | while | flops 399369 | bytes 2771177 | solution.py:28
  1554.0 37.9 %while.249 = (s32[]{:T(128)}, f32[12,128,64]{2,1,0:T(8,128)}, f32[12,128]{1,0:T(8,128)}, s32[]{:T(128)}, f32[4,12,128,64]{2,3,1,0:T(8,128)}, /*index=5*/f32[4]{0...) while((s32[]{:T(128)}, f32[12,128,64]{2,1,0:T(8,128)}, ...), condition=%wide.region_246.247_spmd.clone, body=%wide.region_245.246_spmd.clone.sunk | while | flops 399365 | bytes 2771115 | solution.py:28
  1629.6 8.8 all-gather.40
  1660.2 38.0 %while.250 = (s32[]{:T(128)}, f32[12,128,64]{2,1,0:T(8,128)}, f32[12,128]{1,0:T(8,128)}, s32[]{:T(128)}, f32[4,12,128,64]{2,3,1,0:T(8,128)}, /*index=5*/f32[4]{0...) while((s32[]{:T(128)}, f32[12,128,64]{2,1,0:T(8,128)}, ...), condition=%wide.region_256.257_spmd.clone, body=%wide.region_255.256_spmd.clone.sunk | while | flops 399369 | bytes 2771177 | solution.py:28
  1750.7 23.1 add_bitcast_fusion.1
  1777.2 8.9 all-gather.41
  1786.1 22.9 add_bitcast_fusion
  1808.9 38.0 %while.251 = (s32[]{:T(128)}, f32[12,128,64]{2,1,0:T(8,128)}, f32[12,128]{1,0:T(8,128)}, s32[]{:T(128)}, f32[4,12,128,64]{2,3,1,0:T(8,128)}, /*index=5*/f32[4]{0...) while((s32[]{:T(128)}, f32[12,128,64]{2,1,0:T(8,128)}, ...), condition=%wide.region_280.281_spmd.clone, body=%wide.region_279.280_spmd.clone.sunk | while | flops 399369 | bytes 2771177 | solution.py:28
  1861.6 17.9 add_bitcast_fusion.2
  1906.0 82.9 %all-reduce.12 = (f32[1,768]{1,0:T(1,128)}, f32[1,768]{1,0:T(1,128)}, f32[1,2304]{1,0:T(1,128)}, f32[1,768]{1,0:T(1,128)}, f32[1,768]{1,0:T(1,128)}, /*index=5*/...) all-reduce(f32[1,768]{1,0:T(1,128)} %broadcast_in_dim.217, ...), channel_id=1, replica_groups=mesh['section'=2,'dp'=4,'ctx'=4] {'dp','ctx'}, use_global_device_ids=true, to_apply=%region_299.300 | all-reduce | flops 9984 | bytes 79872 | tf_op jit(solution)/shard_map/psum | solution.py:394
  1994.2 633.8 %all-reduce.17.cloned.1.call-done = (f32[1,768,2304]{2,1,0:T(8,128)}, f32[1,64,768]{2,1,0:T(8,128)}, f32[1,64,768]{2,1,0:T(8,128)}, f32[1,768,768]{2,1,0:T(8,128...) async-done(((f32[1,768,2304]{2,1,0:T(8,128)}, f32[1,64,768]{2,1,0:T(8,128)}, f32[1,64,768]{2,1,0:T(8,128)}, f32[1,768,768]{2,1,0:T(8,128)}, f32[1,768,3072]{2,1,0:T(8,128)}, ...) | async-done | bytes 28704784 | tf_op jit(solution)/shard_map/psum | solution.py:394
  2637.4 9.3 copy.1210
  (2664 shorter events, 1681.2 us)
Async XLA Ops:
  7.2 160.3 %all-gather.57.cloned.1.call-start = ((), (), s32[]{:S(2)}) async-start(), calls=%async_computation | async-start | bytes 1966080 | tf_op jit(solution)/shard_map/all_gather | solution.py:15
  52.6 37.2 %copy-start.581 = (f32[128]{0:T(128)}, f32[128]{0:T(128)S(1)}, u32[]{:S(2)}) copy-start(f32[128]{0:T(128)S(1)} %eq.432) | copy-start | bytes 1540
  54.6 35.3 %copy-start.612 = (f32[128]{0:T(128)}, f32[128]{0:T(128)S(1)}, u32[]{:S(2)}) copy-start(f32[128]{0:T(128)S(1)} %reshape.3252) | copy-start | bytes 1540
  72.4 225.5 %all-gather.59.cloned.1.call-start = ((), (), s32[]{:S(2)}) async-start(), calls=%async_computation.1 | async-start | bytes 1966080 | tf_op jit(solution)/shard_map/all_gather | solution.py:15
  108.2 25.8 copy-start.733
  219.0 2.7 collective-permute-start
  266.5 154.3 %all-gather.61.cloned.1.call-start = ((), (), s32[]{:S(2)}) async-start(), calls=%async_computation.2 | async-start | bytes 1966080 | tf_op jit(solution)/shard_map/all_gather | solution.py:15
  367.4 107.6 %collective-permute-start.2 = (bf16[128,768]{1,0:T(8,128)(2,1)}, bf16[128,768]{1,0:T(8,128)(2,1)}, u32[]{:S(2)}, u32[]{:S(2)}) collective-permute-start(bf16[128,768]{1,0:T(8,128)(2,1)} %get-tuple-element.3504), channel_id=1, source_target_pairs={{0,16},{1,17},{2,18},{3,19},{4,20},{5,21},{6,22},{7,23},{8,24},{9,... | collective-permute-start | bytes 589832 | tf_op jit(solution)/shard_map/ppermute | solution.py:34
  389.6 162.9 %all-gather.63.cloned.1.call-start = ((), (), s32[]{:S(2)}) async-start(), calls=%async_computation.3 | async-start | bytes 1966080 | tf_op jit(solution)/shard_map/all_gather | solution.py:15
  475.4 3.3 collective-permute-start.1
  521.4 142.8 %all-gather.65.cloned.1.call-start = ((), (), s32[]{:S(2)}) async-start(), calls=%async_computation.4 | async-start | bytes 1966080 | tf_op jit(solution)/shard_map/all_gather | solution.py:15
  621.6 99.3 %collective-permute-start.4 = (bf16[128,768]{1,0:T(8,128)(2,1)}, bf16[128,768]{1,0:T(8,128)(2,1)}, u32[]{:S(2)}, u32[]{:S(2)}) collective-permute-start(bf16[128,768]{1,0:T(8,128)(2,1)} %get-tuple-element.3506), channel_id=1, source_target_pairs={{0,16},{1,17},{2,18},{3,19},{4,20},{5,21},{6,22},{7,23},{8,24},{9,... | collective-permute-start | bytes 589832 | tf_op jit(solution)/shard_map/ppermute | solution.py:34
  632.9 163.8 %all-gather.67.cloned.1.call-start = ((), (), s32[]{:S(2)}) async-start(), calls=%async_computation.5 | async-start | bytes 1966080 | tf_op jit(solution)/shard_map/all_gather | solution.py:15
  718.1 3.5 collective-permute-start.3
  765.5 143.2 %all-gather.69.cloned.1.call-start = ((), (), s32[]{:S(2)}) async-start(), calls=%async_computation.6 | async-start | bytes 1966080 | tf_op jit(solution)/shard_map/all_gather | solution.py:15
  866.3 99.5 %collective-permute-start.6 = (bf16[128,768]{1,0:T(8,128)(2,1)}, bf16[128,768]{1,0:T(8,128)(2,1)}, u32[]{:S(2)}, u32[]{:S(2)}) collective-permute-start(bf16[128,768]{1,0:T(8,128)(2,1)} %get-tuple-element.3508), channel_id=1, source_target_pairs={{0,16},{1,17},{2,18},{3,19},{4,20},{5,21},{6,22},{7,23},{8,24},{9,... | collective-permute-start | bytes 589832 | tf_op jit(solution)/shard_map/ppermute | solution.py:34
  877.5 164.0 %all-gather.71.cloned.1.call-start = ((), (), s32[]{:S(2)}) async-start(), calls=%async_computation.7 | async-start | bytes 1966080 | tf_op jit(solution)/shard_map/all_gather | solution.py:15
  962.9 3.5 collective-permute-start.5
  1010.4 143.0 %all-gather.73.cloned.1.call-start = ((), (), s32[]{:S(2)}) async-start(), calls=%async_computation.8 | async-start | bytes 1966080 | tf_op jit(solution)/shard_map/all_gather | solution.py:15
  1110.9 99.6 %collective-permute-start.8 = (bf16[128,768]{1,0:T(8,128)(2,1)}, bf16[128,768]{1,0:T(8,128)(2,1)}, u32[]{:S(2)}, u32[]{:S(2)}) collective-permute-start(bf16[128,768]{1,0:T(8,128)(2,1)} %get-tuple-element.3510), channel_id=1, source_target_pairs={{0,16},{1,17},{2,18},{3,19},{4,20},{5,21},{6,22},{7,23},{8,24},{9,... | collective-permute-start | bytes 589832 | tf_op jit(solution)/shard_map/ppermute | solution.py:34
  1122.1 164.2 %all-gather.75.cloned.1.call-start = ((), (), s32[]{:S(2)}) async-start(), calls=%async_computation.9 | async-start | bytes 1966080 | tf_op jit(solution)/shard_map/all_gather | solution.py:15
  1207.6 3.5 collective-permute-start.7
  1255.2 142.7 %all-gather.77.cloned.1.call-start = ((), (), s32[]{:S(2)}) async-start(), calls=%async_computation.10 | async-start | bytes 1966080 | tf_op jit(solution)/shard_map/all_gather | solution.py:15
  1355.4 100.5 %collective-permute-start.10 = (bf16[128,768]{1,0:T(8,128)(2,1)}, bf16[128,768]{1,0:T(8,128)(2,1)}, u32[]{:S(2)}, u32[]{:S(2)}) collective-permute-start(bf16[128,768]{1,0:T(8,128)(2,1)} %get-tuple-element.3512), channel_id=1, source_target_pairs={{0,16},{1,17},{2,18},{3,19},{4,20},{5,21},{6,22},{7,23},{8,24},{9,... | collective-permute-start | bytes 589832 | tf_op jit(solution)/shard_map/ppermute | solution.py:34
  1366.7 187.3 %all-gather.79.cloned.1.call-start = ((), (), s32[]{:S(2)}) async-start(), calls=%async_computation.11 | async-start | bytes 1966080 | tf_op jit(solution)/shard_map/all_gather | solution.py:15
  1453.1 3.5 collective-permute-start.9
  1519.5 140.7 %all-gather.81.cloned.1.call-start = ((), (), s32[]{:S(2)}) async-start(), calls=%async_computation.12 | async-start | bytes 1966080 | tf_op jit(solution)/shard_map/all_gather | solution.py:15
  1625.3 183.7 %all-gather.83.cloned.1.call-start = ((), (), s32[]{:S(2)}) async-start(), calls=%async_computation.13 | async-start | bytes 1966080 | tf_op jit(solution)/shard_map/all_gather | solution.py:15
  1715.4 3.5 collective-permute-start.11
  1735.3 892.8 %all-reduce.17.cloned.1.call-start = ((), (), s32[]{:S(2)}) async-start(), calls=%async_computation.14 | async-start | bytes 57409536 | tf_op jit(solution)/shard_map/psum | solution.py:394
  1750.7 23.2 copy-start.57
  1750.7 24.1 copy-start.655
  (748 other events, 2915.0 us)
Sparse Core Ops, SparseCore 0:
  72.5 33.9 all-gather.56
  266.7 31.2 all-gather.58
  389.7 31.0 all-gather.60
  521.5 30.9 all-gather.62
  633.0 31.0 all-gather.64
  765.7 30.9 all-gather.66
  877.6 31.0 all-gather.68
  1010.5 30.9 all-gather.70
  1122.2 31.1 all-gather.72
  1255.3 30.9 all-gather.74
  1366.8 31.0 all-gather.76
  1519.7 30.9 all-gather.78
  1625.4 31.0 all-gather.80
  1735.4 31.0 all-gather.82
  1879.6 748.4 all-reduce.16
where the time goes:
time: 2690 us; the launch traced here: 2660 us
  matrix products  756 us (28%)
  waiting for transfers between devices  672 us (25%)
  other arithmetic  462 us (17%)
  local copies, waits for them, and re-layouts  440 us (16%)
  blocking collectives  218 us (8%)
  starting transfers between devices  36.9 us (1%)
  loops' own time  36.8 us (1%)
  between operations  35.8 us (1%)
    psum x1, waiting for transfers between devices, body(): totals = lax.psum(totals, ('dp', 'ctx'))  634 us
    dynamic_slice x168, local copies, waits for them, and re-layouts, step(): new = combine(before, jax.tree.map(lambda part: part[at], everything))  288 us
    select_n x112, other arithmetic, step(): return jax.tree.map(lambda a, b: jnp.where(reached, a, b), new, before)  204 us
    dot_general x28, matrix products, outer_sum(): lax.dot_general(left, right, (((0,), (0,)), ((), ())), preferred_element_...  169 us
    all_gather x14, blocking collectives, prefix(): everything = jax.tree.map(lambda part: lax.all_gather(part, axis), shard)  125 us
    dot_general x42, matrix products, matmul(): return jnp.dot(left, right, preferred_element_type=jnp.float32)  108 us
    psum x1, blocking collectives, body(): totals = lax.psum(totals, ('dp', 'ctx'))  82.9 us
    unnamed x1537, local copies, waits for them, and re-layouts  82 us
  transfers between devices with their start and end apart: 27, of which 17 were waited for; matrix products, arithmetic and copies ran while one was open for 28% of the time, Pallas kernels for 0%

commit v1 on v0

--- a/solution.py
+++ b/solution.py
@@ -1,6 +1,10 @@
+import functools
+
 import jax
 import jax.numpy as jnp
 from jax import lax
+from jax.experimental import pallas as pl
+from jax.experimental.pallas import tpu as pltpu
 from jax.sharding import PartitionSpec as P
 
 BLOCK = 64
@@ -200,11 +204,11 @@
     ) = saved
     before, trailing, usable, allowed, restart = geometry
     grad_down = grad_out.astype(jnp.bfloat16)
-    down_w_grad = outer_sum(activated, grad_down)
+    down_w_grad = (activated, grad_down)
     down_b_grad = jnp.sum(grad_down.astype(jnp.float32), 0)
     grad_active = times_transposed(grad_down, weights[12])
     grad_hidden = jax.vjp(gelu_tanh, hidden)[1](grad_active)[0].astype(jnp.bfloat16)
-    up_w_grad = outer_sum(normed_two, grad_hidden)
+    up_w_grad = (normed_two, grad_hidden)
     up_b_grad = jnp.sum(grad_hidden.astype(jnp.float32), 0)
     grad_normed_two = times_transposed(grad_hidden, weights[10])
     second_back = jax.vjp(
@@ -212,7 +216,7 @@
     )[1](grad_normed_two)
     grad_residual = grad_out + second_back[0]
     grad_branch = grad_residual.astype(jnp.bfloat16)
-    out_w_grad = outer_sum(attended, grad_branch)
+    out_w_grad = (attended, grad_branch)
     out_b_grad = jnp.sum(grad_branch.astype(jnp.float32), 0)
     head_size = weights[4].shape[0]
     grad_attended = times_transposed(grad_branch, weights[6]).reshape(rows.shape[0], -1, head_size)
@@ -275,7 +279,7 @@
         .reshape(rows.shape[0], -1)
         .astype(jnp.bfloat16)
     )
-    qkv_w_grad = outer_sum(normed, grad_projected)
+    qkv_w_grad = (normed, grad_projected)
     qkv_b_grad = jnp.sum(grad_projected.astype(jnp.float32), 0)
     grad_normed = times_transposed(grad_projected, weights[2])
     first_back = jax.vjp(
@@ -301,13 +305,291 @@
     return (grad_rows, grads)
 
 
+MESH = pl.DeviceIdType.MESH
+WIDE = 768
+HALF = 384
+
+
+def bit_length(size):
+    return (size - 1).bit_length()
+
+
+def bit_orders(ctx_size, dp_size):
+    ctx_bits = [("ctx", k) for k in range(bit_length(ctx_size))]
+    dp_bits = [("dp", k) for k in range(bit_length(dp_size))]
+
+    def interleaved(first, second):
+        order = []
+        for k in range(max(len(first), len(second))):
+            order += first[k : k + 1] + second[k : k + 1]
+        return order
+
+    return (interleaved(ctx_bits, dp_bits), interleaved(ctx_bits[::-1], dp_bits))
+
+
+def halvings(rows, count):
+    sizes, halved = [rows], []
+    for _ in range(count):
+        halved.append(sizes[-1] % 32 == 0)
+        sizes.append(sizes[-1] // 2 if halved[-1] else sizes[-1])
+    return sizes, halved
+
+
+class Reduction:
+    def __init__(self, rows, orders):
+        self.rows, self.orders = rows, orders
+        self.count = len(orders[0])
+        self.sizes, self.halved = halvings(rows, self.count)
+        self.steps = [("rs", s) for s in range(self.count)]
+        self.steps += [("ag", s) for s in reversed(range(self.count)) if self.halved[s]]
+        self.offsets, self.bits = [], []
+        for order in orders:
+            offset, offsets, bits = 0, [0], []
+            for s, (axis, k) in enumerate(order):
+                bit = (lax.axis_index(axis) // (1 << k)) % 2
+                bits.append(bit)
+                if self.halved[s]:
+                    offset = offset + bit * self.sizes[s + 1]
+                offsets.append(offset)
+            self.offsets.append(offsets)
+            self.bits.append(bits)
+
+    def partner(self, part, s):
+        axis, k = self.orders[part][s]
+        return {axis: lax.axis_index(axis) + (1 << k) * (1 - 2 * self.bits[part][s])}
+
+    def rows_at(self, offset, size):
+        if isinstance(offset, int):
+            return pl.ds(offset, size)
+        return pl.ds(pl.multiple_of(offset, 16), size)
+
+    def copy(self, buffer, whole, received, sems, part, step):
+        kind, s = self.steps[step]
+        columns = pl.ds(part * HALF, HALF)
+        size = self.sizes[s + 1]
+        if kind == "rs":
+            offset = self.offsets[part][s]
+            if self.halved[s]:
+                offset = offset + (1 - self.bits[part][s]) * size
+            source = buffer.at[self.rows_at(offset, size), columns]
+            target = received[s]
+        else:
+            source = whole.at[self.rows_at(self.offsets[part][s + 1], size), columns]
+            target = source
+        return pltpu.make_async_remote_copy(
+            src_ref=source,
+            dst_ref=target,
+            send_sem=sems[0],
+            recv_sem=sems[1],
+            device_id=self.partner(part, s),
+            device_id_type=MESH,
+        )
+
+    def add(self, buffer, whole, received, part, step):
+        kind, s = self.steps[step]
+        if kind == "rs":
+            size = self.sizes[s + 1]
+            rows = self.rows_at(self.offsets[part][s + 1], size)
+            columns = pl.ds(part * HALF, HALF)
+            total = buffer[rows, columns].astype(jnp.float32) + received[s][...].astype(jnp.float32)
+            target = whole if s + 1 == self.count else buffer
+            target[rows, columns] = total.astype(jnp.bfloat16)
+
+
+def reduce_kernel(
+    orders, chunks, x_ref, small_ref, qkv_out, out_out, up_out, down_out, small_out, *scratch
+):
+    count = len(orders[0])
+    big, big_whole, little, little_whole = scratch[:4]
+    scratch = scratch[4:]
+    big_recv, little_recv = scratch[:count], scratch[count : 2 * count]
+    left, right, wide, send, recv, send_small, recv_small, load, store = scratch[2 * count :]
+    large, small = Reduction(WIDE, orders), Reduction(little.shape[0], orders)
+    steps = len(large.steps)
+
+    barrier = pltpu.get_barrier_semaphore()
+    for s in range(count):
+        pl.semaphore_signal(barrier, inc=1, device_id=large.partner(0, s), device_id_type=MESH)
+    pl.semaphore_wait(barrier, count)
+
+    def operands(c):
+        left_at = jnp.where(c < 4, c, jnp.where(c < 8, 4, jnp.where(c == 8, 5, 6)))
+        right_at = jnp.where(c < 4, 7, c + 4)
+        slot = c % 2
+        return (
+            pltpu.make_async_copy(x_ref.at[left_at], left.at[slot], load.at[slot, 0]),
+            pltpu.make_async_copy(x_ref.at[right_at], right.at[slot], load.at[slot, 1]),
+        )
+
+    def result(c, kind):
+        slot = c % 2
+        source, sem = wide.at[slot], store.at[slot]
+        if kind == "down":
+            target = down_out.at[pl.ds(pl.multiple_of(c * WIDE, WIDE), WIDE), :]
+        elif kind == "up":
+            target = up_out.at[:, pl.ds(pl.multiple_of((c - 4) * WIDE, WIDE), WIDE)]
+        elif kind == "out":
+            target = out_out
+        else:
+            target = qkv_out.at[:, pl.ds(pl.multiple_of((c - 9) * WIDE, WIDE), WIDE)]
+        return pltpu.make_async_copy(source, target, sem)
+
+    def for_each_kind(c, action):
+        for kind, low, high in (("down", 0, 4), ("up", 4, 8), ("out", 8, 9), ("qkv", 9, 12)):
+            @pl.when((c >= low) & (c < high))
+            def _():
+                action(result(c, kind))
+
+    def big_copy(c, part, step):
+        received = [r.at[c, part] for r in big_recv]
+        sems = (send.at[c, part, step], recv.at[c, part, step])
+        return large.copy(big.at[c], big_whole.at[c], received, sems, part, step)
+
+    def small_copy(part, step):
+        received = [r.at[part] for r in little_recv]
+        sems = (send_small.at[part, step], recv_small.at[part, step])
+        return small.copy(little, little_whole, received, sems, part, step)
+
+    for copy in operands(0):
+        copy.start()
+    little[...] = small_ref[...].astype(jnp.bfloat16)
+    for part in range(2):
+        small_copy(part, 0).start()
+
+    def tick(t, carry):
+        @pl.when(t < chunks)
+        def _():
+            for copy in operands(t):
+                copy.wait()
+
+            @pl.when(t + 1 < chunks)
+            def _():
+                for copy in operands(t + 1):
+                    copy.start()
+
+            slot = t % 2
+            big[t] = lax.dot_general(
+                left[slot],
+                right[slot],
+                (((0,), (0,)), ((), ())),
+                preferred_element_type=jnp.float32,
+            ).astype(jnp.bfloat16)
+            for part in range(2):
+                big_copy(t, part, 0).start()
+
+        for step in range(steps):
+            c = t - 1 - step
+
+            @pl.when((c >= 0) & (c < chunks))
+            def _():
+                for part in range(2):
+                    big_copy(c, part, step).wait()
+                    received = [r.at[c, part] for r in big_recv]
+                    large.add(big.at[c], big_whole.at[c], received, part, step)
+                    if step + 1 < steps:
+                        big_copy(c, part, step + 1).start()
+                if step + 1 == steps:
+                    @pl.when(c >= 2)
+                    def _():
+                        for_each_kind(c - 2, lambda copy: copy.wait())
+
+                    wide[c % 2] = big_whole[c].astype(jnp.float32)
+                    for_each_kind(c, lambda copy: copy.start())
+
+            if step < len(small.steps):
+                @pl.when(t == step)
+                def _():
+                    for part in range(2):
+                        small_copy(part, step).wait()
+                        received = [r.at[part] for r in little_recv]
+                        small.add(little, little_whole, received, part, step)
+                        if step + 1 < len(small.steps):
+                            small_copy(part, step + 1).start()
+
+        return carry
+
+    lax.fori_loop(0, chunks + steps, tick, 0)
+    for c in (chunks - 2, chunks - 1):
+        result(c, "qkv").wait()
+    small_out[...] = little_whole[...].astype(jnp.float32)
+
+
+def reduced(x, small, mesh):
+    orders = bit_orders(mesh.shape["ctx"], mesh.shape["dp"])
+    count, chunks, tokens = len(orders[0]), 12, x.shape[1]
+    sizes, _ = halvings(WIDE, count)
+    small_rows = small.shape[0]
+    small_sizes, small_halved = halvings(small_rows, count)
+    steps = count + sum(halvings(WIDE, count)[1])
+    small_steps = count + sum(small_halved)
+    any_space = pl.BlockSpec(memory_space=pl.ANY)
+    in_vmem = pl.BlockSpec(memory_space=pltpu.VMEM)
+    f32, bf16 = jnp.float32, jnp.bfloat16
+    return pl.pallas_call(
+        functools.partial(reduce_kernel, orders, chunks),
+        out_shape=(
+            jax.ShapeDtypeStruct((WIDE, 3 * WIDE), f32),
+            jax.ShapeDtypeStruct((WIDE, WIDE), f32),
+            jax.ShapeDtypeStruct((WIDE, 4 * WIDE), f32),
+            jax.ShapeDtypeStruct((4 * WIDE, WIDE), f32),
+            jax.ShapeDtypeStruct((small_rows, WIDE), f32),
+        ),
+        in_specs=[any_space, in_vmem],
+        out_specs=(any_space,) * 4 + (in_vmem,),
+        scratch_shapes=[
+            pltpu.VMEM((chunks, WIDE, WIDE), bf16),
+            pltpu.VMEM((chunks, WIDE, WIDE), bf16),
+            pltpu.VMEM((small_rows, WIDE), bf16),
+            pltpu.VMEM((small_rows, WIDE), bf16),
+            *(pltpu.VMEM((chunks, 2, size, HALF), bf16) for size in sizes[1:]),
+            *(pltpu.VMEM((2, size, HALF), bf16) for size in small_sizes[1:]),
+            pltpu.VMEM((2, tokens, WIDE), bf16),
+            pltpu.VMEM((2, tokens, WIDE), bf16),
+            pltpu.VMEM((2, WIDE, WIDE), f32),
+            pltpu.SemaphoreType.DMA((chunks, 2, steps)),
+            pltpu.SemaphoreType.DMA((chunks, 2, steps)),
+            pltpu.SemaphoreType.DMA((2, small_steps)),
+            pltpu.SemaphoreType.DMA((2, small_steps)),
+            pltpu.SemaphoreType.DMA((2, 2)),
+            pltpu.SemaphoreType.DMA((2,)),
+        ],
+        compiler_params=pltpu.CompilerParams(
+            collective_id=0, has_side_effects=True, vmem_limit_bytes=60 * 1024 * 1024
+        ),
+    )(x, small)
+
+
 def select_section(first_section, early, late):
     return jax.tree.map(
         lambda early_leaf, late_leaf: jnp.where(first_section, early_leaf, late_leaf), early, late
     )
 
 
+def sum_up(collected, mesh):
+    wide = {}
+    for index in (2, 6, 10, 12):
+        for side in (0, 1):
+            rows = jnp.concatenate([grads[index][side] for grads in collected])
+            wide[index, side] = [rows[:, k : k + WIDE] for k in range(0, rows.shape[1], WIDE)]
+    x = jnp.stack(
+        wide[12, 0] + wide[10, 0] + wide[6, 0] + wide[2, 0]
+        + wide[12, 1] + wide[10, 1] + wide[6, 1] + wide[2, 1]
+    )
+    narrow = (0, 1, 3, 4, 5, 7, 8, 9, 11, 13)
+    parts = [sum(grads[index] for grads in collected) for index in narrow]
+    flat = jnp.concatenate([part.reshape(-1, WIDE) for part in parts])
+    small = jnp.pad(flat, ((0, 256 - flat.shape[0]), (0, 0)))
+    qkv_grad, out_grad, up_grad, down_grad, small = reduced(x, small, mesh)
+    totals, at = {2: qkv_grad, 6: out_grad, 10: up_grad, 12: down_grad}, 0
+    for index, part in zip(narrow, parts):
+        count = part.size // WIDE
+        totals[index] = small[at : at + count].reshape(part.shape)
+        at += count
+    return tuple(totals[index] for index in range(14))
+
+
 def body(
+    mesh,
     ends_in,
     begins,
     filled,
@@ -370,7 +652,7 @@
         if position < micro_count:
             received = passed_along(output, "section", 1)
     incoming = jnp.zeros(local_rows.shape[1:], jnp.float32)
-    totals = None
+    collected = []
     back_rows = []
     for position in range(micro_count + 1):
         early = max(position - 1, 0)
@@ -388,10 +670,10 @@
         grad_out = jnp.where(first_section, incoming, own_grad)
         grad_rows, grads = block_backward(rows, weights, geometry, carried, grad_out)
         back_rows.append(grad_rows.astype(jnp.bfloat16))
-        totals = grads if totals is None else jax.tree.map(jnp.add, totals, grads)
+        collected.append(grads)
         if position < micro_count:
             incoming = passed_along(back_rows[-1], "section", -1).astype(jnp.float32)
-    totals = lax.psum(totals, ("dp", "ctx"))
+    totals = sum_up(collected, mesh)
     ends_out = jnp.where(first_section, jnp.stack(back_rows[1:]), jnp.stack(produced[1:]))[None]
     return (ends_out,) + tuple((total[None] for total in totals))
 
@@ -417,7 +699,7 @@
         P("section", None),
     )
     return jax.shard_map(
-        body,
+        functools.partial(body, mesh),
         mesh=mesh,
         in_specs=placed,
         out_specs=(

time: 2690 us -> 2220 us (0.83)
  waiting for transfers between devices: 672 us -> 43.4 us
  Pallas kernels: 0 us -> 224 us
  matrix products: 756 us -> 617 us
  local copies, waits for them, and re-layouts: 440 us -> 565 us
  blocking collectives: 218 us -> 132 us
  other arithmetic: 462 us -> 507 us
    psum x1 -> x0, waiting for transfers between devices: 634 us -> none  [body(): totals = lax.psum(totals, ('dp', 'ctx'))]
    pallas_call x0 -> x1, Pallas kernels: none -> 224 us  [reduced(): pl.pallas_call(functools.partial(reduce_kernel, orders, chunks), out_shap...]
    dot_general x28 -> x0, matrix products: 169 us -> none  [outer_sum(): lax.dot_general(left, right, (((0,), (0,)), ((), ())), preferred_element_...]
    psum x1 -> x0, blocking collectives: 82.9 us -> none  [body(): totals = lax.psum(totals, ('dp', 'ctx'))]
    unnamed x1537 -> x1595, local copies, waits for them, and re-layouts: 82 us -> 152 us
    convert_element_type x0 -> x14, local copies, waits for them, and re-layouts: none -> 27.1 us  [the longest x7 14.9 us: block_backward(): grad_projected = jnp.stack([grad_queries, grad_keys, grad_values], 1).res...]
  transfers between devices with their start and end apart: 27 -> 26, of which waited for: 17 -> 8; matrix products, arithmetic and copies ran while one was open for 28% -> 30% of each run, Pallas kernels for 0% -> 0%
where the time goes in v1:
time: 2220 us; the launch traced here: 2190 us
  matrix products  617 us (28%)
  local copies, waits for them, and re-layouts  565 us (25%)
  other arithmetic  507 us (23%)
  Pallas kernels  224 us (10%)
  blocking collectives  132 us (6%)
  waiting for transfers between devices  43.4 us (2%)
  loops' own time  39.3 us (2%)
  between operations  35.8 us (2%)
  starting transfers between devices  22.7 us (1%)
    dynamic_slice x168, local copies, waits for them, and re-layouts, step(): new = combine(before, jax.tree.map(lambda part: part[at], everything))  288 us
    pallas_call x1, Pallas kernels, reduced(): pl.pallas_call(functools.partial(reduce_kernel, orders, chunks), out_shap...  224 us
    select_n x112, other arithmetic, step(): return jax.tree.map(lambda a, b: jnp.where(reached, a, b), new, before)  199 us
    unnamed x1595, local copies, waits for them, and re-layouts  152 us
    dot_general x42, matrix products, matmul(): return jnp.dot(left, right, preferred_element_type=jnp.float32)  126 us
    all_gather x14, blocking collectives, prefix(): everything = jax.tree.map(lambda part: lax.all_gather(part, axis), shard)  122 us
    another operation x62, other arithmetic  80 us
    dot_general x28, matrix products, times_transposed(): lax.dot_general(left, right, (((1,), (1,)), ((), ())), preferred_element_...  79.8 us
  transfers between devices with their start and end apart: 26, of which 8 were waited for; matrix products, arithmetic and copies ran while one was open for 30% of the time, Pallas kernels for 0%

profile of v1, /device:TPU:0, one launch (start us, length us, event | category | flops | bytes accessed | tf_op | source)
XLA Modules:
  0.0 2186.6 jit_solution(15265322465922782484)
XLA Ops:
  116.0 11.0 all-gather.28
  162.2 9.8 all-reduce.13
  190.2 37.7 %while.238 = (s32[]{:T(128)}, f32[12,128,64]{2,1,0:T(8,128)}, f32[12,128]{1,0:T(8,128)}, s32[]{:T(128)}, f32[4,12,128,64]{2,3,1,0:T(8,128)}, /*index=5*/f32[4]{0...) while((s32[]{:T(128)}, f32[12,128,64]{2,1,0:T(8,128)}, f32[12,128]{1,0:T(8,128)}, ...), condition=%wide.region_14.15_spmd.clone, body=%wide.region_13.14_spmd.clone.sunk | while | flops 399365 | bytes 2771115 | solution.py:32
  282.6 8.5 all-gather.29
  322.5 38.1 %while.239 = (s32[]{:T(128)}, f32[12,128,64]{2,1,0:T(8,128)}, f32[12,128]{1,0:T(8,128)}, s32[]{:T(128)}, f32[4,12,128,64]{2,3,1,0:T(8,128)}, /*index=5*/f32[4]{0...) while((s32[]{:T(128)}, f32[12,128,64]{2,1,0:T(8,128)}, f32[12,128]{1,0:T(8,128)}, ...), condition=%wide.region_38.39_spmd.clone, body=%wide.region_37.38_spmd.clone.sunk | while | flops 399365 | bytes 2771115 | solution.py:32
  411.5 8.9 all-gather.30
  436.0 37.9 %while.240 = (s32[]{:T(128)}, f32[12,128,64]{2,1,0:T(8,128)}, f32[12,128]{1,0:T(8,128)}, s32[]{:T(128)}, f32[4,12,128,64]{2,3,1,0:T(8,128)}, /*index=5*/f32[4]{0...) while((s32[]{:T(128)}, f32[12,128,64]{2,1,0:T(8,128)}, ...), condition=%wide.region_48.49_spmd.clone, body=%wide.region_47.48_spmd.clone.sunk | while | flops 399369 | bytes 2771177 | solution.py:32
  543.5 8.8 all-gather.31
  569.5 38.2 %while.241 = (s32[]{:T(128)}, f32[12,128,64]{2,1,0:T(8,128)}, f32[12,128]{1,0:T(8,128)}, s32[]{:T(128)}, f32[4,12,128,64]{2,3,1,0:T(8,128)}, /*index=5*/f32[4]{0...) while((s32[]{:T(128)}, f32[12,128,64]{2,1,0:T(8,128)}, f32[12,128]{1,0:T(8,128)}, ...), condition=%wide.region_80.81_spmd.clone, body=%wide.region_79.80_spmd.clone.sunk | while | flops 399365 | bytes 2771115 | solution.py:32
  674.2 8.5 all-gather.65.cloned.1.call-done
  682.7 37.6 %while.242 = (s32[]{:T(128)}, f32[12,128,64]{2,1,0:T(8,128)}, f32[12,128]{1,0:T(8,128)}, s32[]{:T(128)}, f32[4,12,128,64]{2,3,1,0:T(8,128)}, /*index=5*/f32[4]{0...) while((s32[]{:T(128)}, f32[12,128,64]{2,1,0:T(8,128)}, ...), condition=%wide.region_90.91_spmd.clone, body=%wide.region_89.90_spmd.clone.sunk | while | flops 399369 | bytes 2771177 | solution.py:32
  791.8 8.8 all-gather.33
  817.8 38.1 %while.243 = (s32[]{:T(128)}, f32[12,128,64]{2,1,0:T(8,128)}, f32[12,128]{1,0:T(8,128)}, s32[]{:T(128)}, f32[4,12,128,64]{2,3,1,0:T(8,128)}, /*index=5*/f32[4]{0...) while((s32[]{:T(128)}, f32[12,128,64]{2,1,0:T(8,128)}, ...), condition=%wide.region_122.123_spmd.clone, body=%wide.region_121.122_spmd.clone.sunk | while | flops 399365 | bytes 2771115 | solution.py:32
  906.5 8.4 all-gather.34
  922.7 8.3 all-gather.69.cloned.1.call-done
  931.0 37.5 %while.244 = (s32[]{:T(128)}, f32[12,128,64]{2,1,0:T(8,128)}, f32[12,128]{1,0:T(8,128)}, s32[]{:T(128)}, f32[4,12,128,64]{2,3,1,0:T(8,128)}, /*index=5*/f32[4]{0...) while((s32[]{:T(128)}, f32[12,128,64]{2,1,0:T(8,128)}, ...), condition=%wide.region_132.133_spmd.clone, body=%wide.region_131.132_spmd.clone.sunk | while | flops 399369 | bytes 2771177 | solution.py:32
  1040.0 8.8 all-gather.35
  1066.0 38.2 %while.245 = (s32[]{:T(128)}, f32[12,128,64]{2,1,0:T(8,128)}, f32[12,128]{1,0:T(8,128)}, s32[]{:T(128)}, f32[4,12,128,64]{2,3,1,0:T(8,128)}, /*index=5*/f32[4]{0...) while((s32[]{:T(128)}, f32[12,128,64]{2,1,0:T(8,128)}, ...), condition=%wide.region_164.165_spmd.clone, body=%wide.region_163.164_spmd.clone.sunk | while | flops 399365 | bytes 2771115 | solution.py:32
  1154.6 8.2 all-gather.36
  1170.7 8.4 all-gather.73.cloned.1.call-done
  1179.1 37.4 %while.246 = (s32[]{:T(128)}, f32[12,128,64]{2,1,0:T(8,128)}, f32[12,128]{1,0:T(8,128)}, s32[]{:T(128)}, f32[4,12,128,64]{2,3,1,0:T(8,128)}, /*index=5*/f32[4]{0...) while((s32[]{:T(128)}, f32[12,128,64]{2,1,0:T(8,128)}, ...), condition=%wide.region_174.175_spmd.clone, body=%wide.region_173.174_spmd.clone.sunk | while | flops 399369 | bytes 2771177 | solution.py:32
  1287.9 8.8 all-gather.37
  1313.9 38.0 %while.247 = (s32[]{:T(128)}, f32[12,128,64]{2,1,0:T(8,128)}, f32[12,128]{1,0:T(8,128)}, s32[]{:T(128)}, f32[4,12,128,64]{2,3,1,0:T(8,128)}, /*index=5*/f32[4]{0...) while((s32[]{:T(128)}, f32[12,128,64]{2,1,0:T(8,128)}, ...), condition=%wide.region_206.207_spmd.clone, body=%wide.region_205.206_spmd.clone.sunk | while | flops 399365 | bytes 2771115 | solution.py:32
  1401.2 8.3 all-gather.38
  1421.4 37.8 %while.248 = (s32[]{:T(128)}, f32[12,128,64]{2,1,0:T(8,128)}, f32[12,128]{1,0:T(8,128)}, s32[]{:T(128)}, f32[4,12,128,64]{2,3,1,0:T(8,128)}, /*index=5*/f32[4]{0...) while((s32[]{:T(128)}, f32[12,128,64]{2,1,0:T(8,128)}, ...), condition=%wide.region_216.217_spmd.clone, body=%wide.region_215.216_spmd.clone.sunk | while | flops 399369 | bytes 2771177 | solution.py:32
  1558.5 8.8 all-gather.39
  1583.4 37.9 %while.249 = (s32[]{:T(128)}, f32[12,128,64]{2,1,0:T(8,128)}, f32[12,128]{1,0:T(8,128)}, s32[]{:T(128)}, f32[4,12,128,64]{2,3,1,0:T(8,128)}, /*index=5*/f32[4]{0...) while((s32[]{:T(128)}, f32[12,128,64]{2,1,0:T(8,128)}, ...), condition=%wide.region_246.247_spmd.clone, body=%wide.region_245.246_spmd.clone.sunk | while | flops 399365 | bytes 2771115 | solution.py:32
  1713.7 35.5 %while.250 = (s32[]{:T(128)}, f32[12,128,64]{2,1,0:T(8,128)}, f32[12,128]{1,0:T(8,128)S(1)}, s32[]{:T(128)}, f32[4,12,128,64]{2,3,1,0:T(8,128)}, /*index=5*/f32[...) while((s32[]{:T(128)}, f32[12,128,64]{2,1,0:T(8,128)}, ...), condition=%wide.region_256.257_spmd.clone, body=%wide.region_255.256_spmd.clone.sunk | while | flops 399369 | bytes 2771177 | solution.py:32
  1802.9 8.7 all-gather.41
  1842.8 35.6 %while.251 = (s32[]{:T(128)}, f32[12,128,64]{2,1,0:T(8,128)}, f32[12,128]{1,0:T(8,128)S(1)}, s32[]{:T(128)}, f32[4,12,128,64]{2,3,1,0:T(8,128)}, /*index=5*/f32[...) while((s32[]{:T(128)}, f32[12,128,64]{2,1,0:T(8,128)}, ...), condition=%wide.region_280.281_spmd.clone, body=%wide.region_279.280_spmd.clone.sunk | while | flops 399369 | bytes 2771177 | solution.py:32
  1923.8 224.3 %shard_map.280 = (f32[768,2304]{1,0:T(8,128)}, f32[768,768]{1,0:T(8,128)}, f32[768,3072]{1,0:T(8,128)}, f32[3072,768]{1,0:T(8,128)}, f32[256,768]{1,0:T(8,128)}) custom-call(bf16[16,896,768]{2,1,0:T(8,128)(2,1)} %fusion.385.x_ref, f32[256,768]{1,0:T(8,128)} %pad.4.small_ref), custom_call_target="tpu_custom_call" | custom-call | tf_op jit(solution)/shard_map/pallas_call | solution.py:528
  2166.6 9.3 copy.1316
  (2737 shorter events, 1737.2 us)
Async XLA Ops:
  7.2 183.0 %all-gather.57.cloned.1.call-start = ((), (), s32[]{:S(2)}) async-start(), calls=%async_computation | async-start | bytes 1966080 | tf_op jit(solution)/shard_map/all_gather | solution.py:19
  91.2 231.3 %all-gather.59.cloned.1.call-start = ((), (), s32[]{:S(2)}) async-start(), calls=%async_computation.1 | async-start | bytes 1966080 | tf_op jit(solution)/shard_map/all_gather | solution.py:19
  241.8 2.8 collective-permute-start
  291.1 144.9 %all-gather.61.cloned.1.call-start = ((), (), s32[]{:S(2)}) async-start(), calls=%async_computation.2 | async-start | bytes 1966080 | tf_op jit(solution)/shard_map/all_gather | solution.py:19
  398.7 93.0 %collective-permute-start.2 = (bf16[128,768]{1,0:T(8,128)(2,1)}, bf16[128,768]{1,0:T(8,128)(2,1)}, u32[]{:S(2)}, u32[]{:S(2)}) collective-permute-start(bf16[128,768]{1,0:T(8,128)(2,1)} %get-tuple-element.3508), channel_id=1, source_target_pairs={{0,16},{1,17},{2,18},{3,19},{4,20},{5,21},{6,22},{7,23},{8,24},{9,... | collective-permute-start | bytes 589832 | tf_op jit(solution)/shard_map/ppermute | solution.py:38
  404.7 164.8 %all-gather.63.cloned.1.call-start = ((), (), s32[]{:S(2)}) async-start(), calls=%async_computation.3 | async-start | bytes 1966080 | tf_op jit(solution)/shard_map/all_gather | solution.py:19
  493.3 3.3 collective-permute-start.1
  533.4 149.3 %all-gather.65.cloned.1.call-start = ((), (), s32[]{:S(2)}) async-start(), calls=%async_computation.4 | async-start | bytes 1966080 | tf_op jit(solution)/shard_map/all_gather | solution.py:19
  645.8 98.4 %collective-permute-start.4 = (bf16[128,768]{1,0:T(8,128)(2,1)}, bf16[128,768]{1,0:T(8,128)(2,1)}, u32[]{:S(2)}, u32[]{:S(2)}) collective-permute-start(bf16[128,768]{1,0:T(8,128)(2,1)} %get-tuple-element.3510), channel_id=1, source_target_pairs={{0,16},{1,17},{2,18},{3,19},{4,20},{5,21},{6,22},{7,23},{8,24},{9,... | collective-permute-start | bytes 589832 | tf_op jit(solution)/shard_map/ppermute | solution.py:38
  651.3 166.5 %all-gather.67.cloned.1.call-start = ((), (), s32[]{:S(2)}) async-start(), calls=%async_computation.5 | async-start | bytes 1966080 | tf_op jit(solution)/shard_map/all_gather | solution.py:19
  739.8 4.4 collective-permute-start.3
  781.7 149.3 %all-gather.69.cloned.1.call-start = ((), (), s32[]{:S(2)}) async-start(), calls=%async_computation.6 | async-start | bytes 1966080 | tf_op jit(solution)/shard_map/all_gather | solution.py:19
  894.1 98.4 %collective-permute-start.6 = (bf16[128,768]{1,0:T(8,128)(2,1)}, bf16[128,768]{1,0:T(8,128)(2,1)}, u32[]{:S(2)}, u32[]{:S(2)}) collective-permute-start(bf16[128,768]{1,0:T(8,128)(2,1)} %get-tuple-element.3512), channel_id=1, source_target_pairs={{0,16},{1,17},{2,18},{3,19},{4,20},{5,21},{6,22},{7,23},{8,24},{9,... | collective-permute-start | bytes 589832 | tf_op jit(solution)/shard_map/ppermute | solution.py:38
  899.6 166.4 %all-gather.71.cloned.1.call-start = ((), (), s32[]{:S(2)}) async-start(), calls=%async_computation.7 | async-start | bytes 1966080 | tf_op jit(solution)/shard_map/all_gather | solution.py:19
  988.0 4.4 collective-permute-start.5
  1029.8 149.3 %all-gather.73.cloned.1.call-start = ((), (), s32[]{:S(2)}) async-start(), calls=%async_computation.8 | async-start | bytes 1966080 | tf_op jit(solution)/shard_map/all_gather | solution.py:19
  1142.2 98.2 %collective-permute-start.8 = (bf16[128,768]{1,0:T(8,128)(2,1)}, bf16[128,768]{1,0:T(8,128)(2,1)}, u32[]{:S(2)}, u32[]{:S(2)}) collective-permute-start(bf16[128,768]{1,0:T(8,128)(2,1)} %get-tuple-element.3514), channel_id=1, source_target_pairs={{0,16},{1,17},{2,18},{3,19},{4,20},{5,21},{6,22},{7,23},{8,24},{9,... | collective-permute-start | bytes 589832 | tf_op jit(solution)/shard_map/ppermute | solution.py:38
  1147.7 166.2 %all-gather.75.cloned.1.call-start = ((), (), s32[]{:S(2)}) async-start(), calls=%async_computation.9 | async-start | bytes 1966080 | tf_op jit(solution)/shard_map/all_gather | solution.py:19
  1236.0 4.4 collective-permute-start.7
  1277.7 143.6 %all-gather.77.cloned.1.call-start = ((), (), s32[]{:S(2)}) async-start(), calls=%async_computation.10 | async-start | bytes 1966080 | tf_op jit(solution)/shard_map/all_gather | solution.py:19
  1384.6 98.6 %collective-permute-start.10 = (bf16[128,768]{1,0:T(8,128)(2,1)}, bf16[128,768]{1,0:T(8,128)(2,1)}, u32[]{:S(2)}, u32[]{:S(2)}) collective-permute-start(bf16[128,768]{1,0:T(8,128)(2,1)} %get-tuple-element.3516), channel_id=1, source_target_pairs={{0,16},{1,17},{2,18},{3,19},{4,20},{5,21},{6,22},{7,23},{8,24},{9,... | collective-permute-start | bytes 589832 | tf_op jit(solution)/shard_map/ppermute | solution.py:38
  1390.2 193.2 %all-gather.79.cloned.1.call-start = ((), (), s32[]{:S(2)}) async-start(), calls=%async_computation.11 | async-start | bytes 1966080 | tf_op jit(solution)/shard_map/all_gather | solution.py:19
  1478.7 4.5 collective-permute-start.9
  1542.2 171.5 %all-gather.81.cloned.1.call-start = ((), (), s32[]{:S(2)}) async-start(), calls=%async_computation.12 | async-start | bytes 1966080 | tf_op jit(solution)/shard_map/all_gather | solution.py:19
  1583.4 42.3 %copy-start.647 = (f32[128]{0:T(128)S(1)}, f32[128]{0:T(128)}, u32[]{:S(2)}) copy-start(f32[128]{0:T(128)} %compare_convert_fusion) | copy-start | bytes 1540
  1680.1 162.6 %all-gather.83.cloned.1.call-start = ((), (), s32[]{:S(2)}) async-start(), calls=%async_computation.13 | async-start | bytes 1966080 | tf_op jit(solution)/shard_map/all_gather | solution.py:19
  1768.8 5.6 collective-permute-start.11
  1923.7 229.2 %copy-start.738 = (f32[128]{0:T(128)S(1)}, f32[128]{0:T(128)}, u32[]{:S(2)}) copy-start(f32[128]{0:T(128)} %get-tuple-element.2854) | copy-start | bytes 1540
  1923.7 230.4 %copy-start.48 = (bf16[128,768]{1,0:T(8,128)(2,1)S(1)}, bf16[128,768]{1,0:T(8,128)(2,1)}, u32[]{:S(2)}) copy-start(bf16[128,768]{1,0:T(8,128)(2,1)} %get-tuple-element.3212) | copy-start | bytes 589828
  1923.7 230.4 %copy-start.582 = (f32[128]{0:T(128)S(1)}, f32[128]{0:T(128)}, u32[]{:S(2)}) copy-start(f32[128]{0:T(128)} %copy-done.580) | copy-start | bytes 1540
  1923.7 230.4 %copy-start.626 = (f32[128]{0:T(128)S(1)}, f32[128]{0:T(128)}, u32[]{:S(2)}) copy-start(f32[128]{0:T(128)} %copy-done.625) | copy-start | bytes 1540
  1923.7 230.4 %copy-start.684 = (f32[128]{0:T(128)S(1)}, f32[128]{0:T(128)}, u32[]{:S(2)}) copy-start(f32[128]{0:T(128)} %copy-done.683) | copy-start | bytes 1540
  (756 other events, 3078.2 us)
Sparse Core Ops, SparseCore 0:
  91.4 33.7 all-gather.56
  291.2 31.2 all-gather.58
  404.8 31.1 all-gather.60
  533.5 31.0 all-gather.62
  651.4 31.1 all-gather.64
  781.8 31.9 all-gather.66
  899.7 31.2 all-gather.68
  1029.9 31.9 all-gather.70
  1147.9 31.1 all-gather.72
  1277.9 31.9 all-gather.74
  1390.3 31.0 all-gather.76
  1542.3 32.0 all-gather.78
  1680.2 30.8 all-gather.80
  1811.7 30.9 all-gather.82

commit v2 on v1

v2 whole, which is shorter than its diff:
```python
import functools

import jax
import jax.numpy as jnp
from jax import lax
from jax.experimental import pallas as pl
from jax.experimental.pallas import tpu as pltpu
from jax.sharding import PartitionSpec as P

BLOCK = 64
ROWS = 128
HEADS = 12
PAIRS = 6
EPSILON = 1e-05
F32, BF16 = jnp.float32, jnp.bfloat16

MESH = pl.DeviceIdType.MESH
WIDE = 768
HALF = 384


def bit_length(size):
    return (size - 1).bit_length()


def bit_orders(ctx_size, dp_size):
    ctx_bits = [("ctx", k) for k in range(bit_length(ctx_size))]
    dp_bits = [("dp", k) for k in range(bit_length(dp_size))]

    def interleaved(first, second):
        order = []
        for k in range(max(len(first), len(second))):
            order += first[k : k + 1] + second[k : k + 1]
        return order

    return (interleaved(ctx_bits, dp_bits), interleaved(ctx_bits[::-1], dp_bits))


def halvings(rows, count):
    sizes, halved = [rows], []
    for _ in range(count):
        halved.append(sizes[-1] % 32 == 0)
        sizes.append(sizes[-1] // 2 if halved[-1] else sizes[-1])
    return sizes, halved


class Reduction:
    def __init__(self, rows, orders):
        self.rows, self.orders = rows, orders
        self.count = len(orders[0])
        self.sizes, self.halved = halvings(rows, self.count)
        self.steps = [("rs", s) for s in range(self.count)]
        self.steps += [("ag", s) for s in reversed(range(self.count)) if self.halved[s]]
        self.offsets, self.bits = [], []
        for order in orders:
            offset, offsets, bits = 0, [0], []
            for s, (axis, k) in enumerate(order):
                bit = (lax.axis_index(axis) // (1 << k)) % 2
                bits.append(bit)
                if self.halved[s]:
                    offset = offset + bit * self.sizes[s + 1]
                offsets.append(offset)
            self.offsets.append(offsets)
            self.bits.append(bits)

    def partner(self, part, s):
        axis, k = self.orders[part][s]
        return {axis: lax.axis_index(axis) + (1 << k) * (1 - 2 * self.bits[part][s])}

    def rows_at(self, offset, size):
        if isinstance(offset, int):
            return pl.ds(offset, size)
        return pl.ds(pl.multiple_of(offset, 16), size)

    def copy(self, buffer, whole, received, sems, part, step):
        kind, s = self.steps[step]
        columns = pl.ds(part * HALF, HALF)
        size = self.sizes[s + 1]
        if kind == "rs":
            offset = self.offsets[part][s]
            if self.halved[s]:
                offset = offset + (1 - self.bits[part][s]) * size
            source = buffer.at[self.rows_at(offset, size), columns]
            target = received[s]
        else:
            source = whole.at[self.rows_at(self.offsets[part][s + 1], size), columns]
            target = source
        return pltpu.make_async_remote_copy(
            src_ref=source,
            dst_ref=target,
            send_sem=sems[0],
            recv_sem=sems[1],
            device_id=self.partner(part, s),
            device_id_type=MESH,
        )

    def add(self, buffer, whole, received, part, step):
        kind, s = self.steps[step]
        if kind == "rs":
            size = self.sizes[s + 1]
            rows = self.rows_at(self.offsets[part][s + 1], size)
            columns = pl.ds(part * HALF, HALF)
            total = buffer[rows, columns].astype(jnp.float32) + received[s][...].astype(jnp.float32)
            target = whole if s + 1 == self.count else buffer
            target[rows, columns] = total.astype(jnp.bfloat16)


def reduce_kernel(
    orders, chunks, x_ref, small_ref, qkv_out, out_out, up_out, down_out, small_out, *scratch
):
    count = len(orders[0])
    big, big_whole, little, little_whole = scratch[:4]
    scratch = scratch[4:]
    big_recv, little_recv = scratch[:count], scratch[count : 2 * count]
    left, right, wide, send, recv, send_small, recv_small, load, store = scratch[2 * count :]
    large, small = Reduction(WIDE, orders), Reduction(little.shape[0], orders)
    steps = len(large.steps)

    barrier = pltpu.get_barrier_semaphore()
    for s in range(count):
        pl.semaphore_signal(barrier, inc=1, device_id=large.partner(0, s), device_id_type=MESH)
    pl.semaphore_wait(barrier, count)

    def operands(c):
        left_at = jnp.where(c < 4, c, jnp.where(c < 8, 4, jnp.where(c == 8, 5, 6)))
        right_at = jnp.where(c < 4, 7, c + 4)
        slot = c % 2
        return (
            pltpu.make_async_copy(x_ref.at[left_at], left.at[slot], load.at[slot, 0]),
            pltpu.make_async_copy(x_ref.at[right_at], right.at[slot], load.at[slot, 1]),
        )

    def result(c, kind):
        slot = c % 2
        source, sem = wide.at[slot], store.at[slot]
        if kind == "down":
            target = down_out.at[pl.ds(pl.multiple_of(c * WIDE, WIDE), WIDE), :]
        elif kind == "up":
            target = up_out.at[:, pl.ds(pl.multiple_of((c - 4) * WIDE, WIDE), WIDE)]
        elif kind == "out":
            target = out_out
        else:
            target = qkv_out.at[:, pl.ds(pl.multiple_of((c - 9) * WIDE, WIDE), WIDE)]
        return pltpu.make_async_copy(source, target, sem)

    def for_each_kind(c, action):
        for kind, low, high in (("down", 0, 4), ("up", 4, 8), ("out", 8, 9), ("qkv", 9, 12)):
            @pl.when((c >= low) & (c < high))
            def _():
                action(result(c, kind))

    def big_copy(c, part, step):
        received = [r.at[c, part] for r in big_recv]
        sems = (send.at[c, part, step], recv.at[c, part, step])
        return large.copy(big.at[c], big_whole.at[c], received, sems, part, step)

    def small_copy(part, step):
        received = [r.at[part] for r in little_recv]
        sems = (send_small.at[part, step], recv_small.at[part, step])
        return small.copy(little, little_whole, received, sems, part, step)

    for copy in operands(0):
        copy.start()
    little[...] = small_ref[...].astype(jnp.bfloat16)
    for part in range(2):
        small_copy(part, 0).start()

    def tick(t, carry):
        @pl.when(t < chunks)
        def _():
            for copy in operands(t):
                copy.wait()

            @pl.when(t + 1 < chunks)
            def _():
                for copy in operands(t + 1):
                    copy.start()

            slot = t % 2
            big[t] = lax.dot_general(
                left[slot],
                right[slot],
                (((0,), (0,)), ((), ())),
                preferred_element_type=jnp.float32,
            ).astype(jnp.bfloat16)
            for part in range(2):
                big_copy(t, part, 0).start()

        for step in range(steps):
            c = t - 1 - step

            @pl.when((c >= 0) & (c < chunks))
            def _():
                for part in range(2):
                    big_copy(c, part, step).wait()
                    received = [r.at[c, part] for r in big_recv]
                    large.add(big.at[c], big_whole.at[c], received, part, step)
                    if step + 1 < steps:
                        big_copy(c, part, step + 1).start()
                if step + 1 == steps:
                    @pl.when(c >= 2)
                    def _():
                        for_each_kind(c - 2, lambda copy: copy.wait())

                    wide[c % 2] = big_whole[c].astype(jnp.float32)
                    for_each_kind(c, lambda copy: copy.start())

            if step < len(small.steps):
                @pl.when(t == step)
                def _():
                    for part in range(2):
                        small_copy(part, step).wait()
                        received = [r.at[part] for r in little_recv]
                        small.add(little, little_whole, received, part, step)
                        if step + 1 < len(small.steps):
                            small_copy(part, step + 1).start()

        return carry

    lax.fori_loop(0, chunks + steps, tick, 0)
    for c in (chunks - 2, chunks - 1):
        result(c, "qkv").wait()
    small_out[...] = little_whole[...].astype(jnp.float32)


def reduced(x, small, mesh):
    orders = bit_orders(mesh.shape["ctx"], mesh.shape["dp"])
    count, chunks, tokens = len(orders[0]), 12, x.shape[1]
    sizes, _ = halvings(WIDE, count)
    small_rows = small.shape[0]
    small_sizes, small_halved = halvings(small_rows, count)
    steps = count + sum(halvings(WIDE, count)[1])
    small_steps = count + sum(small_halved)
    any_space = pl.BlockSpec(memory_space=pl.ANY)
    in_vmem = pl.BlockSpec(memory_space=pltpu.VMEM)
    f32, bf16 = jnp.float32, jnp.bfloat16
    return pl.pallas_call(
        functools.partial(reduce_kernel, orders, chunks),
        out_shape=(
            jax.ShapeDtypeStruct((WIDE, 3 * WIDE), f32),
            jax.ShapeDtypeStruct((WIDE, WIDE), f32),
            jax.ShapeDtypeStruct((WIDE, 4 * WIDE), f32),
            jax.ShapeDtypeStruct((4 * WIDE, WIDE), f32),
            jax.ShapeDtypeStruct((small_rows, WIDE), f32),
        ),
        in_specs=[any_space, in_vmem],
        out_specs=(any_space,) * 4 + (in_vmem,),
        scratch_shapes=[
            pltpu.VMEM((chunks, WIDE, WIDE), bf16),
            pltpu.VMEM((chunks, WIDE, WIDE), bf16),
            pltpu.VMEM((small_rows, WIDE), bf16),
            pltpu.VMEM((small_rows, WIDE), bf16),
            *(pltpu.VMEM((chunks, 2, size, HALF), bf16) for size in sizes[1:]),
            *(pltpu.VMEM((2, size, HALF), bf16) for size in small_sizes[1:]),
            pltpu.VMEM((2, tokens, WIDE), bf16),
            pltpu.VMEM((2, tokens, WIDE), bf16),
            pltpu.VMEM((2, WIDE, WIDE), f32),
            pltpu.SemaphoreType.DMA((chunks, 2, steps)),
            pltpu.SemaphoreType.DMA((chunks, 2, steps)),
            pltpu.SemaphoreType.DMA((2, small_steps)),
            pltpu.SemaphoreType.DMA((2, small_steps)),
            pltpu.SemaphoreType.DMA((2, 2)),
            pltpu.SemaphoreType.DMA((2,)),
        ],
        compiler_params=pltpu.CompilerParams(
            collective_id=0, has_side_effects=True, vmem_limit_bytes=60 * 1024 * 1024
        ),
    )(x, small)


def dot_nn(left, right):
    return jnp.dot(left, right, preferred_element_type=F32)


def dot_nt(left, right):
    return lax.dot_general(left, right, (((1,), (1,)), ((), ())), preferred_element_type=F32)


def dot_tn(left, right):
    return lax.dot_general(left, right, (((0,), (0,)), ((), ())), preferred_element_type=F32)


def high_low(values):
    high = values.astype(BF16)
    return high, (values - high.astype(F32)).astype(BF16)


def tile(index, size):
    return pl.ds(pl.multiple_of(index * size, size), size)


def loop(count, step, unroll=1):
    def body(k, carry):
        step(k)
        return carry

    lax.fori_loop(0, count, body, 0, unroll=unroll)


def low_lanes(rows):
    return lax.broadcasted_iota(jnp.int32, (rows, 128), 1) < 64


def normalised(rows):
    average = jnp.mean(rows, -1, keepdims=True)
    centred = rows - average
    scale = lax.rsqrt(jnp.mean(centred * centred, -1, keepdims=True) + EPSILON)
    return centred * scale, scale


def norm_input_grad(grad, standard, scale, gain):
    wide = grad * gain
    first = jnp.mean(wide, -1, keepdims=True)
    second = jnp.mean(wide * standard, -1, keepdims=True)
    return scale * (wide - first - standard * second)


def half_sums(values, low):
    first = jnp.sum(jnp.where(low, values, 0.0), -1, keepdims=True)
    second = jnp.sum(jnp.where(low, 0.0, values), -1, keepdims=True)
    return jnp.where(low, first, second)


def half_softmax(logits, low, ones):
    lowest = jnp.float32(-3e38)
    first = jnp.max(jnp.where(low, logits, lowest), -1, keepdims=True)
    second = jnp.max(jnp.where(low, lowest, logits), -1, keepdims=True)
    powers = jnp.exp(logits - jnp.where(low, first, second))
    high, rest = high_low(powers)
    return powers / dot_nn(jnp.concatenate([high, rest], 1), jnp.concatenate([ones, ones], 0))


def layers_kernel(ctx_size, *refs):
    (
        x_in, meta, first_gain, first_shift, qkv_w, qkv_b, map_q, map_k, pair_q, pair_k,
        out_w, out_b, second_gain, second_shift, up_w, up_b, down_w, down_b,
        x_out, ends, small,
        rows, grad_in, normed, proj, phi_q, phi_k, att, att_wide, den, res, act, slope,
        states, back_state, back_in, back_out, grad_wide, branch,
        ones, mask, mask_t, bef, trail, x_sem, in_sem, out_sem, remote,
    ) = refs
    section, me = lax.axis_index("section"), lax.axis_index("ctx")
    has_before = (6 * me) % ctx_size != 0
    has_after = (6 * (me + 1)) % ctx_size != 0
    reach = (6 * me + 5) % ctx_size
    shift = jnp.where(reach <= 5, 5 - reach, 0)
    other = {"section": 1 - section}

    def remote_copy(source, target, index, device):
        return pltpu.make_async_remote_copy(
            src_ref=source,
            dst_ref=target,
            send_sem=remote.at[index, 0],
            recv_sem=remote.at[index, 1],
            device_id=device,
            device_id_type=MESH,
        )

    forward_rows = remote_copy(branch, rows, 0, other)
    backward_rows = remote_copy(rows, grad_in, 1, other)
    state_on = remote_copy(states.at[6], states.at[0], 2, {"ctx": me + 1})
    state_back = remote_copy(back_out, back_in, 3, {"ctx": me - 1})

    barrier = pltpu.get_barrier_semaphore()
    pl.semaphore_signal(barrier, inc=1, device_id=other, device_id_type=MESH)

    @pl.when(has_before)
    def _():
        pl.semaphore_signal(barrier, inc=1, device_id={"ctx": me - 1}, device_id_type=MESH)

    @pl.when(has_after)
    def _():
        pl.semaphore_signal(barrier, inc=1, device_id={"ctx": me + 1}, device_id_type=MESH)

    pl.semaphore_wait(barrier, 1 + has_before.astype(jnp.int32) + has_after.astype(jnp.int32))

    @pl.when(section == 0)
    def _():
        copy = pltpu.make_async_copy(x_in, rows, in_sem)
        copy.start()
        copy.wait()

    @pl.when(section == 1)
    def _():
        copy = pltpu.make_async_copy(x_in, grad_in, in_sem)
        copy.start()

    def put(source, index):
        pltpu.make_async_copy(source, x_out.at[index], x_sem.at[index]).start()

    def put_done(source, index):
        pltpu.make_async_copy(source, x_out.at[index], x_sem.at[index]).wait()

    low = low_lanes(ROWS)
    row_of = lax.broadcasted_iota(jnp.int32, (ROWS, 128), 0).astype(F32)
    lane_of = lax.broadcasted_iota(jnp.int32, (ROWS, 128), 1).astype(F32)
    ones[...] = ((row_of < 64) == (lane_of < 64)).astype(BF16)
    small[...] = jnp.zeros_like(small)

    def usable(tokens, filled_first, filled_second):
        return jnp.where(
            tokens < 64, (tokens < filled_first).astype(F32), (tokens - 64 < filled_second).astype(F32)
        )

    def prepare(j):
        start_first, start_second = meta[j, 0:1, :], meta[j, 1:2, :]
        filled_first, filled_second = meta[j, 2:3, :], meta[j, 3:4, :]
        cut = ((row_of >= 64) & (lane_of < 64)).astype(F32) * start_second
        seen = (lane_of <= row_of).astype(F32) * (1.0 - cut)
        mask[...] = seen * usable(lane_of, filled_first, filled_second)
        cut = ((lane_of >= 64) & (row_of < 64)).astype(F32) * start_second
        seen = (row_of <= lane_of).astype(F32) * (1.0 - cut)
        of_rows = usable(row_of, filled_first, filled_second)
        mask_t[...] = seen * of_rows
        kept = 1.0 - start_first
        bef[...] = jnp.where(row_of < 64, kept, kept * (1.0 - start_second)).astype(BF16)
        tail = jnp.where(row_of < 64, 1.0 - start_second, jnp.ones_like(start_second))
        trail[...] = (tail * of_rows).astype(BF16)
        return kept * (1.0 - start_second)

    @pl.when(jnp.logical_not(has_before))
    def _():
        states[0] = jnp.zeros_like(states[0])

    @pl.when(shift != 0)
    def _():
        states[shift] = jnp.zeros_like(states[0])

    @pl.when(section == 1)
    def _():
        forward_rows.wait_recv()

    def first_norm(k):
        at = tile(k, ROWS)
        standard, _ = normalised(rows[at, :].astype(F32))
        normed[at, :] = (standard * first_gain[...].astype(F32) + first_shift[...].astype(F32)).astype(BF16)

    loop(6, first_norm)

    def project(k):
        at = tile(k, 256)
        proj[:, at] = (dot_nn(normed[...], qkv_w[:, at]) + qkv_b[:, at].astype(F32)).astype(BF16)

    loop(9, project)
    put(normed, 6)

    def features(k):
        at = tile(k % 6, ROWS)
        p = k // 6
        for source, table, target in ((0, map_q, phi_q), (6, map_k, phi_k)):
            logits = dot_nn(proj[at, tile(source + p, 128)], table[p])
            for half in range(2):
                phi = half_softmax(logits[:, half * 128 : half * 128 + 128], low, ones[...])
                target[at, tile(2 * p + half, 128)] = phi.astype(BF16)

    loop(36, features)

    def attend(k):
        j = (shift + k) % 6

        @pl.when((j == 0) & has_before)
        def _():
            state_on.wait_recv()

        keep = prepare(j)
        at = tile(j, ROWS)

        def pair(p):
            values = proj[at, tile(12 + p, 128)]
            results = []
            for half in range(2):
                h = 2 * p + half
                own = low if half == 0 else jnp.logical_not(low)
                extended = jnp.where(own, values, jnp.ones_like(values))
                queries, keys = phi_q[at, tile(h, 128)], phi_k[at, tile(h, 128)]
                high, rest = high_low(dot_nt(queries, keys) * mask[...])
                state = states[j, h]
                state_high, state_low = high_low(state)
                early = queries * bef[...]
                results.append(
                    dot_nn(
                        jnp.concatenate([high, rest, early, early], 1),
                        jnp.concatenate([extended, extended, state_high, state_low], 0),
                    )
                )
                states[j + 1, h] = keep * state + dot_tn(keys * trail[...], extended)
            top = jnp.where(low, results[0], results[1])
            bottom = pltpu.roll(jnp.where(low, results[1], results[0]), 64, 1)
            share = top / bottom
            att_wide[at, tile(p, 128)] = share
            den[at, tile(p, 128)] = bottom
            att[at, tile(p, 128)] = share.astype(BF16)

        loop(PAIRS, pair)

        @pl.when((j == 5) & has_after)
        def _():
            state_on.start()

    loop(6, attend)
    put(att, 5)

    def branch_out(k):
        at = tile(k, 256)
        total = dot_nn(att[...], out_w[:, at]) + out_b[:, at].astype(F32)
        res[:, at] = rows[:, at].astype(F32) + total

    loop(3, branch_out)
    put_done(normed, 6)

    def second_norm(k):
        at = tile(k, ROWS)
        standard, _ = normalised(res[at, :])
        normed[at, :] = (standard * second_gain[...].astype(F32) + second_shift[...].astype(F32)).astype(BF16)

    loop(6, second_norm)
    put(normed, 4)

    def feed(k):
        at, rows_at = tile(k // 3, 256), tile(k % 3, 256)
        hidden = dot_nn(normed[rows_at, :], up_w[:, at]) + up_b[:, at].astype(F32)
        square = hidden * hidden
        inner = 0.7978845608028654 * hidden * (1.0 + 0.044715 * square)
        bent = jnp.tanh(inner)
        half = 0.5 * (1.0 + bent)
        act[rows_at, at] = (hidden * half).astype(BF16)
        steep = 0.7978845608028654 * (1.0 + 3.0 * 0.044715 * square)
        slope[rows_at, at] = (half + 0.5 * hidden * (1.0 - bent * bent) * steep).astype(BF16)

    loop(36, feed)
    for n in range(4):
        put(act.at[:, pl.ds(n * WIDE, WIDE)], n)

    def settle(k):
        at = tile(k, 256)
        total = res[:, at] + dot_nn(act[...], down_w[:, at]) + down_b[:, at].astype(F32)
        branch[:, at] = total.astype(BF16)

    loop(3, settle)

    @pl.when(section == 0)
    def _():
        forward_rows.start()
        forward_rows.wait_send()
        backward_rows.wait_recv()

    @pl.when(section == 1)
    def _():
        pltpu.make_async_copy(x_in, grad_in, in_sem).wait()
        copy = pltpu.make_async_copy(branch, ends, out_sem)
        copy.start()
        copy.wait()

    put(grad_in, 7)

    def column_sums(values):
        return jnp.sum(values.astype(F32), 0, keepdims=True)

    small[140:141, :] = column_sums(grad_in[...])

    def feed_back(k):
        at = tile(k, 256)
        grads = dot_nt(grad_in[...], down_w[at, :])
        grads = (grads * slope[:, at].astype(F32)).astype(BF16)
        slope[:, at] = grads

    loop(12, feed_back)
    for n in range(4):
        put(slope.at[:, pl.ds(n * WIDE, WIDE)], 8 + n)
        small[136 + n : 137 + n, :] = column_sums(slope[:, n * WIDE : n * WIDE + WIDE])

    def second_grad(k):
        at = tile(k, 256)
        grad_wide[:, at] = dot_nt(slope[...], up_w[at, :])

    loop(3, second_grad)

    def second_back(k):
        at = tile(k, ROWS)
        grads = grad_wide[at, :]
        standard, scale = normalised(res[at, :])
        small[134:135, :] += jnp.sum(grads * standard, 0, keepdims=True)
        small[135:136, :] += jnp.sum(grads, 0, keepdims=True)
        grads = norm_input_grad(grads, standard, scale, second_gain[...].astype(F32))
        grads = grad_in[at, :].astype(F32) + grads
        res[at, :] = grads
        rounded = grads.astype(BF16)
        branch[at, :] = rounded
        small[133:134, :] += column_sums(rounded)

    loop(6, second_back)
    put(branch, 12)

    def attended_grad(k):
        at = tile(k, 256)
        grad_wide[:, at] = dot_nt(branch[...], out_w[at, :])

    loop(3, attended_grad)
    for n in range(4):
        put_done(act.at[:, pl.ds(n * WIDE, WIDE)], n)

    put_done(att, 5)
    back_state[...] = jnp.zeros_like(back_state)

    def attend_back(k):
        j = (shift + 5 - k) % 6

        @pl.when(j == 5)
        def _():
            @pl.when(has_after)
            def _():
                state_back.wait_recv()
                back_state[...] = back_in[...]

            @pl.when(jnp.logical_not(has_after))
            def _():
                back_state[...] = jnp.zeros_like(back_state)

        keep = prepare(j)
        at = tile(j, ROWS)

        def pair(p):
            values = proj[at, tile(12 + p, 128)]
            grads = (grad_wide[at, tile(p, 128)] / den[at, tile(p, 128)]).astype(BF16)
            sums = -half_sums(grads.astype(F32) * att_wide[at, tile(p, 128)], low)
            other_sums = pltpu.roll(sums, 64, 1)
            lanes = lax.broadcasted_iota(jnp.int32, (ROWS, 128), 1) % 64
            one = other_sums.astype(BF16).astype(F32)
            two = (other_sums - one).astype(BF16).astype(F32)
            three = other_sums - one - two
            spread = jnp.where(lanes == 0, one, jnp.where(lanes == 1, two, jnp.where(lanes == 2, three, 0.0)))
            spread = spread.astype(BF16)
            value_grads, query_grads, key_grads = [], [], []
            for half in range(2):
                h = 2 * p + half
                own = low if half == 0 else jnp.logical_not(low)
                extended = jnp.where(own, values, jnp.ones_like(values))
                grads_ext = jnp.where(own, grads, spread)
                queries, keys = phi_q[at, tile(h, 128)], phi_k[at, tile(h, 128)]
                high, rest = high_low(dot_nt(grads_ext, extended) * mask[...])
                state_high, state_low = high_low(states[j, h])
                query_grad = dot_nn(
                    jnp.concatenate([high, rest], 1), jnp.concatenate([keys, keys], 0)
                )
                query_grad += bef[...].astype(F32) * dot_nt(
                    jnp.concatenate([grads_ext, grads_ext], 1),
                    jnp.concatenate([state_high, state_low], 1),
                )
                high, rest = high_low(dot_nt(extended, grads_ext) * mask_t[...])
                later = back_state[h]
                later_high, later_low = high_low(later)
                key_grad = dot_nn(
                    jnp.concatenate([high, rest], 1), jnp.concatenate([queries, queries], 0)
                )
                key_grad += trail[...].astype(F32) * dot_nt(
                    jnp.concatenate([extended, extended], 1),
                    jnp.concatenate([later_high, later_low], 1),
                )
                scores_t = (dot_nt(keys, queries) * mask_t[...]).astype(BF16)
                value_grads.append(
                    dot_nn(
                        jnp.concatenate([scores_t, keys * trail[...]], 1),
                        jnp.concatenate([grads_ext, later_high], 0),
                    )
                )
                back_state[h] = keep * later + dot_tn(queries * bef[...], grads_ext)
                for phi, grad, kept in ((queries, query_grad, query_grads), (keys, key_grad, key_grads)):
                    phi = phi.astype(F32)
                    kept.append(phi * (grad - half_sums(phi * grad, low)))
            act[at, tile(12 + p, 128)] = jnp.where(low, value_grads[0], value_grads[1]).astype(BF16)
            for kept, target, first in ((query_grads, act, 18), (key_grads, att, 0)):
                left = kept[0] - pltpu.roll(kept[0], 64, 1)
                right = pltpu.roll(kept[1], 64, 1) - kept[1]
                target[at, tile(first + p, 128)] = jnp.where(low, left, right).astype(BF16)

        loop(PAIRS, pair)

        @pl.when((j == 0) & has_before)
        def _():
            back_out[...] = back_state[...]
            state_back.start()

    loop(6, attend_back)

    def maps_back(p):
        lanes = tile(p, 128)
        first = lax.broadcasted_iota(jnp.int32, (64, 128), 1) < 64
        for offset, target, source, table, at in ((0, act, 18, pair_q, 0), (6, att, 0, pair_k, 64)):
            logit_grads = target[:, tile(source + p, 128)]
            act[:, tile(offset + p, 128)] = dot_nt(logit_grads, table[p]).astype(BF16)
            product = dot_tn(proj[:, tile(offset + p, 128)], logit_grads)
            small[at : at + 64, lanes] = jnp.where(first, product[:64], product[64:])

    loop(PAIRS, maps_back)
    for n in range(3):
        put(act.at[:, pl.ds(n * WIDE, WIDE)], 13 + n)
        small[130 + n : 131 + n, :] = column_sums(act[:, n * WIDE : n * WIDE + WIDE])

    def first_grad(k):
        at = tile(k, 256)
        grad_wide[:, at] = dot_nt(act[:, : 3 * WIDE], qkv_w[at, :])

    loop(3, first_grad)

    def first_back(k):
        at = tile(k, ROWS)
        grads = grad_wide[at, :]
        standard, scale = normalised(rows[at, :].astype(F32))
        small[128:129, :] += jnp.sum(grads * standard, 0, keepdims=True)
        small[129:130, :] += jnp.sum(grads, 0, keepdims=True)
        grads = norm_input_grad(grads, standard, scale, first_gain[...].astype(F32))
        rows[at, :] = (res[at, :] + grads).astype(BF16)

    loop(6, first_back)

    @pl.when(section == 1)
    def _():
        backward_rows.start()
        backward_rows.wait_send()

    @pl.when(section == 0)
    def _():
        copy = pltpu.make_async_copy(rows, ends, out_sem)
        copy.start()
        copy.wait()

    put_done(normed, 4)
    put_done(grad_in, 7)
    put_done(branch, 12)
    for n in range(4):
        put_done(slope.at[:, pl.ds(n * WIDE, WIDE)], 8 + n)
    for n in range(3):
        put_done(act.at[:, pl.ds(n * WIDE, WIDE)], 13 + n)

    @pl.when(has_after)
    def _():
        state_on.wait_send()

    @pl.when(has_before)
    def _():
        state_back.wait_send()


def layers(x_in, meta, weights, mesh):
    (
        first_gain, first_shift, qkv_w, qkv_b, query_map, key_map, out_w, out_b,
        second_gain, second_shift, up_w, up_b, down_w, down_b,
    ) = weights

    def tables(table):
        heads = table.reshape(64, PAIRS, 2, 64).transpose(1, 2, 0, 3)
        both = jnp.concatenate([heads, -heads], -1)
        none, zero = jnp.zeros_like(both[:, 0]), jnp.zeros_like(heads[:, 0])
        signed = jnp.concatenate(
            [
                jnp.concatenate([both[:, 0], none], -1),
                jnp.concatenate([none, both[:, 1]], -1),
            ],
            1,
        )
        plain = jnp.concatenate(
            [
                jnp.concatenate([heads[:, 0], zero], -1),
                jnp.concatenate([zero, heads[:, 1]], -1),
            ],
            1,
        )
        return signed, plain

    map_q, pair_q = tables(query_map[0])
    map_k, pair_k = tables(key_map[0])
    tokens = 6 * ROWS
    any_space = pl.BlockSpec(memory_space=pl.ANY)
    in_vmem = pl.BlockSpec(memory_space=pltpu.VMEM)
    return pl.pallas_call(
        functools.partial(layers_kernel, mesh.shape["ctx"]),
        out_shape=(
            jax.ShapeDtypeStruct((16, tokens, WIDE), BF16),
            jax.ShapeDtypeStruct((tokens, WIDE), BF16),
            jax.ShapeDtypeStruct((256, WIDE), F32),
        ),
        in_specs=[any_space] + [in_vmem] * 17,
        out_specs=(any_space, any_space, in_vmem),
        scratch_shapes=[
            pltpu.VMEM((tokens, WIDE), BF16),
            pltpu.VMEM((tokens, WIDE), BF16),
            pltpu.VMEM((tokens, WIDE), BF16),
            pltpu.VMEM((tokens, 3 * WIDE), BF16),
            pltpu.VMEM((tokens, 2 * WIDE), BF16),
            pltpu.VMEM((tokens, 2 * WIDE), BF16),
            pltpu.VMEM((tokens, WIDE), BF16),
            pltpu.VMEM((tokens, WIDE), F32),
            pltpu.VMEM((tokens, WIDE), F32),
            pltpu.VMEM((tokens, WIDE), F32),
            pltpu.VMEM((tokens, 4 * WIDE), BF16),
            pltpu.VMEM((tokens, 4 * WIDE), BF16),
            pltpu.VMEM((7, HEADS, 128, 128), F32),
            pltpu.VMEM((HEADS, 128, 128), F32),
            pltpu.VMEM((HEADS, 128, 128), F32),
            pltpu.VMEM((HEADS, 128, 128), F32),
            pltpu.VMEM((tokens, WIDE), F32),
            pltpu.VMEM((tokens, WIDE), BF16),
            pltpu.VMEM((128, 128), BF16),
            pltpu.VMEM((128, 128), F32),
            pltpu.VMEM((128, 128), F32),
            pltpu.VMEM((128, 128), BF16),
            pltpu.VMEM((128, 128), BF16),
            pltpu.SemaphoreType.DMA((16,)),
            pltpu.SemaphoreType.DMA,
            pltpu.SemaphoreType.DMA,
            pltpu.SemaphoreType.DMA((4, 2)),
        ],
        compiler_params=pltpu.CompilerParams(
            collective_id=1, has_side_effects=True, vmem_limit_bytes=60 * 1024 * 1024
        ),
    )(
        x_in.reshape(tokens, WIDE), meta, first_gain, first_shift, qkv_w[0], qkv_b, map_q, map_k,
        pair_q, pair_k, out_w[0], out_b, second_gain, second_shift, up_w[0], up_b, down_w[0], down_b,
    )


def move_kernel(ctx_size, gather, count, *refs):
    sources, targets, sems = refs[:count], refs[count : 2 * count], refs[2 * count]
    me = lax.axis_index("ctx")
    barrier = pltpu.get_barrier_semaphore()

    def greet(k):
        device = {"ctx": (me + 1 + k) % ctx_size}
        pl.semaphore_signal(barrier, inc=1, device_id=device, device_id_type=MESH)

    loop(ctx_size - 1, greet)
    pl.semaphore_wait(barrier, ctx_size - 1)

    def place(k):
        if gather:
            at = k * ctx_size + me
            return at // 6, at % 6
        at = 6 * me + k
        return at % ctx_size, at // ctx_size

    def origin(k):
        if gather:
            return (6 * me + k) % ctx_size
        return (k * ctx_size + me) // 6

    def local(n, k, at):
        return pltpu.make_async_copy(sources[n].at[k], targets[n].at[at], sems.at[n, 2, k])

    def remote(n, k, at, device):
        return pltpu.make_async_remote_copy(
            src_ref=sources[n].at[k],
            dst_ref=targets[n].at[at],
            send_sem=sems.at[n, 0, k],
            recv_sem=sems.at[n, 1, at],
            device_id={"ctx": device},
            device_id_type=MESH,
        )

    for n in range(count):
        for k in range(6):
            device, at = place(k)

            @pl.when(device == me)
            def _():
                local(n, k, at).start()

            @pl.when(device != me)
            def _():
                remote(n, k, at, device).start()

    for n in range(count):
        for k in range(6):
            device, at = place(k)

            @pl.when(device == me)
            def _():
                local(n, k, at).wait()

            @pl.when(device != me)
            def _():
                remote(n, k, at, device).wait_send()

            @pl.when(origin(k) != me)
            def _():
                remote(n, k, k, (me + 1) % ctx_size).wait_recv()


def moved(arrays, mesh, gather):
    count = len(arrays)
    in_vmem = pl.BlockSpec(memory_space=pltpu.VMEM)
    return pl.pallas_call(
        functools.partial(move_kernel, mesh.shape["ctx"], gather, count),
        out_shape=tuple(jax.ShapeDtypeStruct(a.shape, a.dtype) for a in arrays),
        in_specs=[in_vmem] * count,
        out_specs=(in_vmem,) * count,
        scratch_shapes=[pltpu.SemaphoreType.DMA((count, 3, 6))],
        compiler_params=pltpu.CompilerParams(
            collective_id=2 if gather else 3, has_side_effects=True, vmem_limit_bytes=16 * 1024 * 1024
        ),
    )(*arrays)


def body(mesh, ends_in, begins, filled, *weights):
    meta = jnp.concatenate([begins, filled], 1).astype(F32)[:, :, None]
    meta = jnp.broadcast_to(jnp.pad(meta, ((0, 0), (0, 4), (0, 0))), (6, 8, 128))
    x_in, meta = moved((ends_in[0], meta), mesh, True)
    x, ends, small = layers(x_in, meta, weights, mesh)
    (ends_out,) = moved((ends.reshape(6, ROWS, WIDE),), mesh, False)
    qkv_grad, out_grad, up_grad, down_grad, small = reduced(x, small, mesh)

    def row(first, count=1):
        return small[first : first + count].reshape(1, count * WIDE)

    return (
        ends_out[None], row(128), row(129), qkv_grad[None], row(130, 3), small[None, :64],
        small[None, 64:128], out_grad[None], row(133), row(134), row(135), up_grad[None],
        row(136, 4), down_grad[None], row(140),
    )


def solution(mesh):
    placed = (
        P("section", None, ("dp", "ctx"), None),
        P(None, ("dp", "ctx")),
        P(None, ("dp", "ctx")),
        P("section", None),
        P("section", None),
        P("section", None, None),
        P("section", None),
        P("section", None, None),
        P("section", None, None),
        P("section", None, None),
        P("section", None),
        P("section", None),
        P("section", None),
        P("section", None, None),
        P("section", None),
        P("section", None, None),
        P("section", None),
    )
    return jax.shard_map(
        functools.partial(body, mesh),
        mesh=mesh,
        in_specs=placed,
        out_specs=(
            P("section", None, ("dp", "ctx"), None),
            P("section", None),
            P("section", None),
            P("section", None, None),
            P("section", None),
            P("section", None, None),
            P("section", None, None),
            P("section", None, None),
            P("section", None),
            P("section", None),
            P("section", None),
            P("section", None, None),
            P("section", None),
            P("section", None, None),
            P("section", None),
        ),
        check_vma=False,
    )
```

time: 2220 us -> 519 us (0.23); the launches traced: 2190 us -> 518 us
  matrix products: 617 us -> 0 us
  local copies, waits for them, and re-layouts: 565 us -> 31.7 us
  other arithmetic: 507 us -> 2.98 us
  Pallas kernels: 224 us -> 483 us
  blocking collectives: 132 us -> 0 us
  waiting for transfers between devices: 43.4 us -> 0 us
  loops' own time: 39.3 us -> 0 us
  between operations: 35.8 us -> 0.81 us
  starting transfers between devices: 22.7 us -> 0 us
    dot_general x224 -> x0, matrix products: 471 us -> none  [the longest x42 126 us: matmul(): return jnp.dot(left, right, preferred_element_type=jnp.float32)]
    pallas_call x0 -> x3, Pallas kernels: none -> 325 us  [the longest x1 288 us: layers(): pl.pallas_call(functools.partial(layers_kernel, mesh.shape['ctx']), out_s...]
    dynamic_slice x168 -> x0, local copies, waits for them, and re-layouts: 288 us -> none  [step(): new = combine(before, jax.tree.map(lambda part: part[at], everything))]
    select_n x124 -> x0, other arithmetic: 215 us -> none  [the longest x112 199 us: step(): return jax.tree.map(lambda a, b: jnp.where(reached, a, b), new, before)]
    sub x56 -> x0, matrix products: 146 us -> none  [the longest x28 72.9 us: feature_map(): jax.nn.softmax(-logits, -1)]
    unnamed x1595 -> x32, local copies, waits for them, and re-layouts: 152 us -> 26.1 us
    all_gather x14 -> x0, blocking collectives: 122 us -> none  [prefix(): everything = jax.tree.map(lambda part: lax.all_gather(part, axis), shard)]
    reduce_sum x94 -> x0, other arithmetic: 82.7 us -> none  [the longest x7 15.1 us: block_backward(): down_b_grad = jnp.sum(grad_down.astype(jnp.float32), 0)]
  transfers between devices with their start and end apart: 26 -> 0, of which waited for: 8 -> 0; matrix products, arithmetic and copies ran while one was open for 30% -> 0% of each run, Pallas kernels for 0% -> 0%
where the time goes in v2:
time: 519 us; the launch traced here: 518 us
  Pallas kernels  483 us (93%)
  local copies, waits for them, and re-layouts  31.7 us (6%)
    pallas_call x1, Pallas kernels, layers(): pl.pallas_call(functools.partial(layers_kernel, mesh.shape['ctx']), out_s...  288 us
    pallas_call x1, Pallas kernels, reduced(): pl.pallas_call(functools.partial(reduce_kernel, orders, chunks), out_shap...  158 us
    pallas_call x2, Pallas kernels, moved(): pl.pallas_call(functools.partial(move_kernel, mesh.shape['ctx'], gather,...  37.2 us
    unnamed x32, local copies, waits for them, and re-layouts  26.1 us

profile of v2, /device:TPU:0, one launch (start us, length us, event | category | flops | bytes accessed | tf_op | source)
XLA Modules:
  0.0 518.4 jit_solution(9421533343767776997)
XLA Ops:
  0.7 0.8 add_convert_fusion
  1.5 0.1 copy.36
  1.6 0.1 broadcast_in_dim.30.refs_1_
  1.6 1.1 reshape_squeeze.6
  2.7 1.1 reshape_squeeze.7
  3.9 0.1 fusion.13
  4.1 0.1 fusion.15
  4.3 0.9 fusion.10
  5.1 1.0 fusion.4
  6.1 22.3 %shard_map.280 = (bf16[6,128,768]{2,1,0:T(8,128)(2,1)S(1)}, f32[6,8,128]{2,1,0:T(8,128)S(1)}) custom-call(bf16[6,128,768]{2,1,0:T(8,128)(2,1)S(1)} %bitcast.55, f32[6,8,128]{2,1,0:T(8,128)S(1)} %broadcast_in_dim.30.refs_1_), custom_call_target="tpu_custom_call" | custom-call | tf_op jit(solution)/shard_map/pallas_call | solution.py:891
  28.5 0.0 copy-start.2
  28.5 1.0 copy-done.2
  29.5 0.6 copy-done.3
  30.1 287.8 %shard_map.281 = (bf16[16,768,768]{2,1,0:T(8,128)(2,1)}, bf16[768,768]{1,0:T(8,128)(2,1)}, f32[256,768]{1,0:T(8,128)}) custom-call(bf16[768,768]{1,0:T(8,128)(2,1)} %bitcast.57, f32[6,8,128]{2,1,0:T(8,128)} %copy-done.3, bf16[1,768]{1,0:T(2,128)(2,1)} %refs_2_.1, bf16[1,768]{1,0:T(2,128)(2,1)} %refs_3_.1, bf16[768,2304]{1,0:T(8,128)(2,1)} %bitcast.67, ...), custom_call_target="tpu_custom_call" | custom-call | tf_op jit(solution)/shard_map/pallas_call | solution.py:775
  317.9 1.3 copy-done.1
  319.2 14.8 %shard_map.282 = bf16[6,128,768]{2,1,0:T(8,128)(2,1)S(1)} custom-call(bf16[6,128,768]{2,1,0:T(8,128)(2,1)S(1)} %bitcast.56), custom_call_target="tpu_custom_call" | custom-call | tf_op jit(solution)/shard_map/pallas_call | solution.py:891
  334.0 157.9 %shard_map.283 = (f32[768,2304]{1,0:T(8,128)}, f32[768,768]{1,0:T(8,128)}, f32[768,3072]{1,0:T(8,128)}, f32[3072,768]{1,0:T(8,128)}, f32[256,768]{1,0:T(8,128)}) custom-call(bf16[16,768,768]{2,1,0:T(8,128)(2,1)} %get-tuple-element.28.x_ref, f32[256,768]{1,0:T(8,128)} %get-tuple-element.29.small_ref), custom_call_target="tpu_custom_call" | custom-call | tf_op jit(solution)/shard_map/pallas_call | solution.py:237
  491.9 0.7 slice_bitcast_fusion.7
  492.7 0.6 copy.37
  493.3 0.7 slice_bitcast_fusion.6
  494.0 0.6 copy.38
  494.7 1.5 fusion.20
  496.2 1.8 slice_bitcast_fusion
  498.0 1.0 copy.52
  499.0 7.6 %copy.53 = f32[1,768,2304]{2,1,0:T(8,128)} copy(f32[1,768,2304]{2,1,0:T(8,128)} %bitcast.64) | data formatting | bytes 14155776
  506.6 1.4 copy.54
  508.0 0.0 slice-start.1
  508.0 0.0 slice-start.2
  508.0 4.8 copy.55
  512.8 1.6 slice-done.1
  514.5 0.2 slice-done.2
  514.7 3.7 copy.56
  (23 shorter events, 0.2 us)
Async XLA Ops:
  0.6 5.5 %copy-start = (bf16[1,6,128,768]{3,2,1,0:T(8,128)(2,1)S(1)}, bf16[1,6,128,768]{3,2,1,0:T(8,128)(2,1)}, u32[]{:S(2)}) copy-start(bf16[1,6,128,768]{3,2,1,0:T(8,128)(2,1)} %param.17) | copy-start | bytes 3538948
  28.5 1.0 copy-start.2
  29.5 0.6 copy-start.3
  317.9 1.3 copy-start.1
  498.0 10.0 %slice-start.3 = ((s8[9437184]{0:T(1024)(128)(4,1)}), s8[4194304]{0:T(1024)(128)(4,1)S(1)}, s32[]{:S(2)}) async-start(s8[9437184]{0:T(1024)(128)(4,1)} %bitcast.61), calls=%async_computation.3 | async-start | bytes 8388608
  499.0 7.6 %copy-start.4 = (f32[768,768]{1,0:T(8,128)S(1)}, f32[768,768]{1,0:T(8,128)}, u32[]{:S(2)}) copy-start(f32[768,768]{1,0:T(8,128)} %get-tuple-element.32) | copy-start | bytes 7077892
  499.0 9.0 %slice-start.4 = ((s8[9437184]{0:T(1024)(128)(4,1)}), s8[4194304]{0:T(1024)(128)(4,1)S(1)}, s32[]{:S(2)}) async-start(s8[9437184]{0:T(1024)(128)(4,1)} %bitcast.61), calls=%async_computation.4 | async-start | bytes 8388608
  499.0 9.0 %slice-start.5 = ((s8[9437184]{0:T(1024)(128)(4,1)}), s8[1048576]{0:T(1024)(128)(4,1)S(1)}, s32[]{:S(2)}) async-start(s8[9437184]{0:T(1024)(128)(4,1)} %bitcast.61), calls=%async_computation.5 | async-start | bytes 2097152
  506.6 6.2 %slice-start = ((s8[9437184]{0:T(1024)(128)(4,1)}), s8[4194304]{0:T(1024)(128)(4,1)S(1)}, s32[]{:S(2)}) async-start(s8[9437184]{0:T(1024)(128)(4,1)} %bitcast.58), calls=%async_computation | async-start | bytes 8388608
  508.0 6.4 %slice-start.1 = ((s8[9437184]{0:T(1024)(128)(4,1)}), s8[4194304]{0:T(1024)(128)(4,1)S(1)}, s32[]{:S(2)}) async-start(s8[9437184]{0:T(1024)(128)(4,1)} %bitcast.58), calls=%async_computation.1 | async-start | bytes 8388608
  508.0 6.7 %slice-start.2 = ((s8[9437184]{0:T(1024)(128)(4,1)}), s8[1048576]{0:T(1024)(128)(4,1)S(1)}, s32[]{:S(2)}) async-start(s8[9437184]{0:T(1024)(128)(4,1)} %bitcast.58), calls=%async_computation.2 | async-start | bytes 2097152

commit v3 on v2

v3 whole, which is shorter than its diff:
```python
import functools

import jax
import jax.numpy as jnp
from jax import lax
from jax.experimental import pallas as pl
from jax.experimental.pallas import tpu as pltpu
from jax.sharding import PartitionSpec as P

BLOCK = 64
ROWS = 128
HEADS = 12
PAIRS = 6
GROUP = 6
GROUP_BACK = 6
EPSILON = 1e-05
F32, BF16 = jnp.float32, jnp.bfloat16

MESH = pl.DeviceIdType.MESH
WIDE = 768
HALF = 384


def bit_length(size):
    return (size - 1).bit_length()


def bit_orders(ctx_size, dp_size):
    ctx_bits = [("ctx", k) for k in range(bit_length(ctx_size))]
    dp_bits = [("dp", k) for k in range(bit_length(dp_size))]

    def interleaved(first, second):
        order = []
        for k in range(max(len(first), len(second))):
            order += first[k : k + 1] + second[k : k + 1]
        return order

    return (interleaved(ctx_bits, dp_bits), interleaved(ctx_bits[::-1], dp_bits))


def halvings(rows, count):
    sizes, halved = [rows], []
    for _ in range(count):
        halved.append(sizes[-1] % 32 == 0)
        sizes.append(sizes[-1] // 2 if halved[-1] else sizes[-1])
    return sizes, halved


class Reduction:
    def __init__(self, rows, orders):
        self.rows, self.orders = rows, orders
        self.count = len(orders[0])
        self.sizes, self.halved = halvings(rows, self.count)
        self.steps = [("rs", s) for s in range(self.count)]
        self.steps += [("ag", s) for s in reversed(range(self.count)) if self.halved[s]]
        self.offsets, self.bits = [], []
        for order in orders:
            offset, offsets, bits = 0, [0], []
            for s, (axis, k) in enumerate(order):
                bit = (lax.axis_index(axis) // (1 << k)) % 2
                bits.append(bit)
                if self.halved[s]:
                    offset = offset + bit * self.sizes[s + 1]
                offsets.append(offset)
            self.offsets.append(offsets)
            self.bits.append(bits)

    def partner(self, part, s):
        axis, k = self.orders[part][s]
        return {axis: lax.axis_index(axis) + (1 << k) * (1 - 2 * self.bits[part][s])}

    def rows_at(self, offset, size):
        if isinstance(offset, int):
            return pl.ds(offset, size)
        return pl.ds(pl.multiple_of(offset, 16), size)

    def copy(self, buffer, whole, received, sems, part, step):
        kind, s = self.steps[step]
        columns = pl.ds(part * HALF, HALF)
        size = self.sizes[s + 1]
        if kind == "rs":
            offset = self.offsets[part][s]
            if self.halved[s]:
                offset = offset + (1 - self.bits[part][s]) * size
            source = buffer.at[self.rows_at(offset, size), columns]
            target = received[s]
        else:
            source = whole.at[self.rows_at(self.offsets[part][s + 1], size), columns]
            target = source
        return pltpu.make_async_remote_copy(
            src_ref=source,
            dst_ref=target,
            send_sem=sems[0],
            recv_sem=sems[1],
            device_id=self.partner(part, s),
            device_id_type=MESH,
        )

    def add(self, buffer, whole, received, part, step):
        kind, s = self.steps[step]
        if kind == "rs":
            size = self.sizes[s + 1]
            rows = self.rows_at(self.offsets[part][s + 1], size)
            columns = pl.ds(part * HALF, HALF)
            total = buffer[rows, columns].astype(jnp.float32) + received[s][...].astype(jnp.float32)
            target = whole if s + 1 == self.count else buffer
            target[rows, columns] = total.astype(jnp.bfloat16)


class Pieces:
    def __init__(self, ctx_size, gather):
        self.size, self.gather, self.me = ctx_size, gather, lax.axis_index("ctx")

    def place(self, k):
        if self.gather:
            at = k * self.size + self.me
            return at // 6, at % 6
        at = 6 * self.me + k
        return at % self.size, at // self.size

    def origin(self, k):
        if self.gather:
            return (6 * self.me + k) % self.size
        return (k * self.size + self.me) // 6

    def start(self, source, target, sems):
        for k in range(6):
            device, at = self.place(k)

            @pl.when(device == self.me)
            def _():
                self.local(source, target, sems, k, at).start()

            @pl.when(device != self.me)
            def _():
                self.remote(source, target, sems, k, at, device).start()

    def wait(self, source, target, sems):
        for k in range(6):
            device, at = self.place(k)

            @pl.when(device == self.me)
            def _():
                self.local(source, target, sems, k, at).wait()

            @pl.when(device != self.me)
            def _():
                self.remote(source, target, sems, k, at, device).wait_send()

            @pl.when(self.origin(k) != self.me)
            def _():
                self.remote(source, target, sems, k, k, (self.me + 1) % self.size).wait_recv()

    def local(self, source, target, sems, k, at):
        return pltpu.make_async_copy(source(k), target(at), sems.at[2, k])

    def remote(self, source, target, sems, k, at, device):
        return pltpu.make_async_remote_copy(
            src_ref=source(k),
            dst_ref=target(at),
            send_sem=sems.at[0, k],
            recv_sem=sems.at[1, at],
            device_id={"ctx": device},
            device_id_type=MESH,
        )


def block_rows(k):
    return pl.ds(k * ROWS if isinstance(k, int) else pl.multiple_of(k * ROWS, ROWS), ROWS)


def greet_ctx(barrier, ctx_size):
    me = lax.axis_index("ctx")

    def greet(k):
        device = {"ctx": (me + 1 + k) % ctx_size}
        pl.semaphore_signal(barrier, inc=1, device_id=device, device_id_type=MESH)

    loop(ctx_size - 1, greet)
    return ctx_size - 1


def reduce_kernel(
    orders, ctx_size, chunks, x_ref, small_ref, ends, sums, small_out, ends_out, *scratch
):
    count = len(orders[0])
    big, big_whole, little, little_whole = scratch[:4]
    scratch = scratch[4:]
    big_recv, little_recv = scratch[:count], scratch[count : 2 * count]
    left, right, send, recv, send_small, recv_small, load, store, moves = scratch[2 * count :]
    large, small = Reduction(WIDE, orders), Reduction(little.shape[0], orders)
    steps = len(large.steps)

    def operands(c):
        left_at = jnp.where(c < 4, c, jnp.where(c < 8, 4, jnp.where(c == 8, 5, 6)))
        right_at = jnp.where(c < 4, 7, c + 4)
        slot = c % 2
        return (
            pltpu.make_async_copy(x_ref.at[left_at], left.at[slot], load.at[slot, 0]),
            pltpu.make_async_copy(x_ref.at[right_at], right.at[slot], load.at[slot, 1]),
        )

    for copy in operands(0):
        copy.start()
    little[...] = small_ref[...].astype(BF16)

    barrier = pltpu.get_barrier_semaphore()
    greeted = greet_ctx(barrier, ctx_size)
    for s in range(count):
        if orders[0][s][0] != "ctx":
            pl.semaphore_signal(barrier, inc=1, device_id=large.partner(0, s), device_id_type=MESH)
            greeted += 1
    pl.semaphore_wait(barrier, greeted)

    def big_copy(c, part, step):
        received = [r.at[c, part] for r in big_recv]
        sems = (send.at[c, part, step], recv.at[c, part, step])
        return large.copy(big.at[c], big_whole.at[c], received, sems, part, step)

    def small_copy(part, step):
        received = [r.at[part] for r in little_recv]
        sems = (send_small.at[part, step], recv_small.at[part, step])
        return small.copy(little, little_whole, received, sems, part, step)

    for part in range(2):
        small_copy(part, 0).start()
    pieces = Pieces(ctx_size, False)
    given = (lambda k: ends.at[block_rows(k), :], lambda k: ends_out.at[k], moves)

    def tick(t, carry):
        @pl.when(t < chunks)
        def _():
            for copy in operands(t):
                copy.wait()

            @pl.when(t + 1 < chunks)
            def _():
                for copy in operands(t + 1):
                    copy.start()

            slot = t % 2
            big[t] = dot_tn(left[slot], right[slot]).astype(BF16)
            for part in range(2):
                big_copy(t, part, 0).start()

        @pl.when(t == chunks)
        def _():
            pieces.start(*given)

        for step in range(steps):
            c = t - 1 - step

            @pl.when((c >= 0) & (c < chunks))
            def _():
                for part in range(2):
                    big_copy(c, part, step).wait()
                    received = [r.at[c, part] for r in big_recv]
                    large.add(big.at[c], big_whole.at[c], received, part, step)
                    if step + 1 < steps:
                        big_copy(c, part, step + 1).start()
                if step + 1 == steps:
                    pltpu.make_async_copy(big_whole.at[c], sums.at[c], store).start()

            if step < len(small.steps):
                @pl.when(t == step)
                def _():
                    for part in range(2):
                        small_copy(part, step).wait()
                        received = [r.at[part] for r in little_recv]
                        small.add(little, little_whole, received, part, step)
                        if step + 1 < len(small.steps):
                            small_copy(part, step + 1).start()

        return carry

    lax.fori_loop(0, chunks + steps, tick, 0)
    small_out[...] = little_whole[...]
    pieces.wait(*given)
    pltpu.make_async_copy(big_whole, sums, store).wait()


def reduced(x, small, ends, mesh):
    orders = bit_orders(mesh.shape["ctx"], mesh.shape["dp"])
    count, chunks, tokens = len(orders[0]), 12, x.shape[1]
    sizes, _ = halvings(WIDE, count)
    small_rows = small.shape[0]
    small_sizes, small_halved = halvings(small_rows, count)
    steps = count + sum(halvings(WIDE, count)[1])
    small_steps = count + sum(small_halved)
    any_space = pl.BlockSpec(memory_space=pl.ANY)
    in_vmem = pl.BlockSpec(memory_space=pltpu.VMEM)
    return pl.pallas_call(
        functools.partial(reduce_kernel, orders, mesh.shape["ctx"], chunks),
        out_shape=(
            jax.ShapeDtypeStruct((chunks, WIDE, WIDE), BF16),
            jax.ShapeDtypeStruct((small_rows, WIDE), BF16),
            jax.ShapeDtypeStruct((6, ROWS, WIDE), BF16),
        ),
        in_specs=[any_space, in_vmem, in_vmem],
        out_specs=(any_space, in_vmem, in_vmem),
        scratch_shapes=[
            pltpu.VMEM((chunks, WIDE, WIDE), BF16),
            pltpu.VMEM((chunks, WIDE, WIDE), BF16),
            pltpu.VMEM((small_rows, WIDE), BF16),
            pltpu.VMEM((small_rows, WIDE), BF16),
            *(pltpu.VMEM((chunks, 2, size, HALF), BF16) for size in sizes[1:]),
            *(pltpu.VMEM((2, size, HALF), BF16) for size in small_sizes[1:]),
            pltpu.VMEM((2, tokens, WIDE), BF16),
            pltpu.VMEM((2, tokens, WIDE), BF16),
            pltpu.SemaphoreType.DMA((chunks, 2, steps)),
            pltpu.SemaphoreType.DMA((chunks, 2, steps)),
            pltpu.SemaphoreType.DMA((2, small_steps)),
            pltpu.SemaphoreType.DMA((2, small_steps)),
            pltpu.SemaphoreType.DMA((2, 2)),
            pltpu.SemaphoreType.DMA,
            pltpu.SemaphoreType.DMA((3, 6)),
        ],
        compiler_params=pltpu.CompilerParams(
            collective_id=0, has_side_effects=True, vmem_limit_bytes=60 * 1024 * 1024
        ),
    )(x, small, ends)


def finish_kernel(sums, little, ends, *refs):
    outs, (narrow, wide, passing, load, store, through) = refs[:15], refs[15:]
    (
        ends_out, first_gain, first_shift, qkv_w, qkv_b, map_q, map_k, out_w, out_b,
        second_gain, second_shift, up_w, up_b, down_w, down_b,
    ) = outs
    take = pltpu.make_async_copy(ends, passing, through.at[0])
    give = pltpu.make_async_copy(passing, ends_out.at[0], through.at[1])
    take.start()
    depth = narrow.shape[0]
    targets = [down_w.at[0, pl.ds(n * WIDE, WIDE), :] for n in range(4)]
    targets += [up_w.at[0, :, pl.ds(n * WIDE, WIDE)] for n in range(4)]
    targets += [out_w.at[0]]
    targets += [qkv_w.at[0, :, pl.ds(n * WIDE, WIDE)] for n in range(3)]

    def read(c):
        return pltpu.make_async_copy(sums.at[c], narrow.at[c % depth], load.at[c % depth])

    def write(c):
        return pltpu.make_async_copy(wide.at[c % depth], targets[c], store.at[c % depth])

    for c in range(depth):
        read(c).start()
    for target, first in (
        (first_gain, 128), (first_shift, 129), (out_b, 133), (second_gain, 134), (second_shift, 135), (down_b, 140),
    ):
        target[...] = little[first : first + 1, :].astype(F32)
    for target, first, count in ((qkv_b, 130, 3), (up_b, 136, 4)):
        for n in range(count):
            target[:, n * WIDE : n * WIDE + WIDE] = little[first + n : first + n + 1, :].astype(F32)
    map_q[0] = little[0:64, :].astype(F32)
    map_k[0] = little[64:128, :].astype(F32)
    take.wait()
    give.start()
    for c in range(len(targets)):
        read(c).wait()
        if c >= depth:
            write(c - depth).wait()

        def widen(k):
            at = tile(k, 256)
            wide[c % depth, at, :] = narrow[c % depth, at, :].astype(F32)

        loop(3, widen)
        write(c).start()
        if c + depth < len(targets):
            read(c + depth).start()
    for c in range(len(targets) - depth, len(targets)):
        write(c).wait()
    give.wait()


def finished(sums, little, ends, weights):
    any_space = pl.BlockSpec(memory_space=pl.ANY)
    in_vmem = pl.BlockSpec(memory_space=pltpu.VMEM)
    shapes = [jax.ShapeDtypeStruct((1,) + ends.shape, BF16)]
    shapes += [jax.ShapeDtypeStruct(weight.shape, F32) for weight in weights]
    large = (0, 3, 7, 11, 13)
    return pl.pallas_call(
        finish_kernel,
        out_shape=tuple(shapes),
        in_specs=[any_space, in_vmem, any_space],
        out_specs=tuple(any_space if n in large else in_vmem for n in range(15)),
        scratch_shapes=[
            pltpu.VMEM((3, WIDE, WIDE), BF16),
            pltpu.VMEM((3, WIDE, WIDE), F32),
            pltpu.VMEM(ends.shape, BF16),
            pltpu.SemaphoreType.DMA((3,)),
            pltpu.SemaphoreType.DMA((3,)),
            pltpu.SemaphoreType.DMA((2,)),
        ],
        compiler_params=pltpu.CompilerParams(vmem_limit_bytes=60 * 1024 * 1024),
    )(sums, little, ends)


def dot_nn(left, right):
    return jnp.dot(left, right, preferred_element_type=F32)


def dot_nt(left, right):
    return lax.dot_general(left, right, (((1,), (1,)), ((), ())), preferred_element_type=F32)


def dot_tn(left, right):
    return lax.dot_general(left, right, (((0,), (0,)), ((), ())), preferred_element_type=F32)


def high_low(values):
    high = values.astype(BF16)
    return high, (values - high.astype(F32)).astype(BF16)


def tile(index, size):
    return pl.ds(pl.multiple_of(index * size, size), size)


def loop(count, step, unroll=1):
    def body(k, carry):
        step(k)
        return carry

    lax.fori_loop(0, count, body, 0, unroll=unroll)


def low_lanes(rows):
    return lax.broadcasted_iota(jnp.int32, (rows, 128), 1) < 64


def normalised(rows):
    average = jnp.mean(rows, -1, keepdims=True)
    centred = rows - average
    scale = lax.rsqrt(jnp.mean(centred * centred, -1, keepdims=True) + EPSILON)
    return centred * scale, scale


def norm_input_grad(grad, standard, scale, gain):
    wide = grad * gain
    first = jnp.mean(wide, -1, keepdims=True)
    second = jnp.mean(wide * standard, -1, keepdims=True)
    return scale * (wide - first - standard * second)


def half_sums(values, low):
    first = jnp.sum(jnp.where(low, values, 0.0), -1, keepdims=True)
    second = jnp.sum(jnp.where(low, 0.0, values), -1, keepdims=True)
    return jnp.where(low, first, second)


def half_softmax(logits, low, ones):
    lowest = jnp.float32(-3e38)
    first = jnp.max(jnp.where(low, logits, lowest), -1, keepdims=True)
    second = jnp.max(jnp.where(low, lowest, logits), -1, keepdims=True)
    powers = jnp.exp(logits - jnp.where(low, first, second))
    high, rest = high_low(powers)
    return powers / dot_nn(jnp.concatenate([high, rest], 1), jnp.concatenate([ones, ones], 0))


def layers_kernel(ctx_size, *refs):
    (
        x_in, begins, filled, first_gain, first_shift, qkv_given, qkv_b, map_q_given, map_k_given,
        out_given, out_b, second_gain, second_shift, up_given, up_b, down_given, down_b,
        x_out, ends, small,
        qkv_w, out_w, up_w, down_w, map_q, map_k, pair_q, pair_k, meta_own, meta,
        rows, grad_in, normed, proj, phi_q, phi_k, att, att_wide, den, res, act, slope,
        states, back_state, back_in, back_out, grad_wide, branch,
        ones, mask, mask_t, bef, trail, x_sem, out_sem, remote, weight_sem, moves,
    ) = refs
    section, me = lax.axis_index("section"), lax.axis_index("ctx")
    has_before = (6 * me) % ctx_size != 0
    has_after = (6 * (me + 1)) % ctx_size != 0
    reach = (6 * me + 5) % ctx_size
    shift = jnp.where(reach <= 5, 5 - reach, 0)
    other = {"section": 1 - section}

    def weight(n):
        given, kept = ((qkv_given, qkv_w), (out_given, out_w), (up_given, up_w), (down_given, down_w))[n]
        return pltpu.make_async_copy(given.at[0], kept, weight_sem.at[n])

    def remote_copy(source, target, index, device):
        return pltpu.make_async_remote_copy(
            src_ref=source,
            dst_ref=target,
            send_sem=remote.at[index, 0],
            recv_sem=remote.at[index, 1],
            device_id=device,
            device_id_type=MESH,
        )

    forward_rows = remote_copy(branch, rows, 0, other)
    backward_rows = remote_copy(rows, grad_in, 1, other)
    state_on = remote_copy(states.at[6], states.at[0], 2, {"ctx": me + 1})
    state_back = remote_copy(back_out, back_in, 3, {"ctx": me - 1})
    pieces = Pieces(ctx_size, True)
    rows_moves = (lambda k: x_in.at[0, k], lambda k: rows.at[block_rows(k), :], moves.at[0])
    grad_moves = (lambda k: x_in.at[0, k], lambda k: grad_in.at[block_rows(k), :], moves.at[0])
    meta_moves = (lambda k: meta_own.at[k], lambda k: meta.at[k], moves.at[1])

    barrier = pltpu.get_barrier_semaphore()
    greeted = greet_ctx(barrier, ctx_size)
    pl.semaphore_signal(barrier, inc=1, device_id=other, device_id_type=MESH)
    for k in range(6):
        for n, source in ((0, begins), (2, filled)):
            for half in range(2):
                value = source[k : k + 1, half : half + 1].astype(F32)
                meta_own[k, n + half : n + half + 1, :] = jnp.broadcast_to(value, (1, 128))
    pl.semaphore_wait(barrier, greeted + 1)

    @pl.when(section == 0)
    def _():
        pieces.start(*rows_moves)

    pieces.start(*meta_moves)
    for n in range(4):
        weight(n).start()

    def put(source, index):
        pltpu.make_async_copy(source, x_out.at[index], x_sem.at[index]).start()

    def put_done(source, index):
        pltpu.make_async_copy(source, x_out.at[index], x_sem.at[index]).wait()

    low = low_lanes(ROWS)
    row_of = lax.broadcasted_iota(jnp.int32, (ROWS, 128), 0).astype(F32)
    lane_of = lax.broadcasted_iota(jnp.int32, (ROWS, 128), 1).astype(F32)
    ones[...] = ((row_of < 64) == (lane_of < 64)).astype(BF16)
    small[...] = jnp.zeros_like(small)
    left_lanes = low_lanes(64)
    for given, signed, plain in ((map_q_given, map_q, pair_q), (map_k_given, map_k, pair_k)):
        signed[...] = jnp.zeros_like(signed)
        for p in range(PAIRS):
            both = given[0, :, p * 128 : p * 128 + 128].astype(F32)
            turned = pltpu.roll(both, 64, 1)
            signed[p, :64, :128] = jnp.where(left_lanes, both, -turned).astype(BF16)
            signed[p, 64:, 128:] = jnp.where(left_lanes, turned, -both).astype(BF16)
            plain[p, :64, :] = jnp.where(left_lanes, both, 0.0).astype(BF16)
            plain[p, 64:, :] = jnp.where(left_lanes, 0.0, both).astype(BF16)

    def usable(tokens, filled_first, filled_second):
        return jnp.where(
            tokens < 64, (tokens < filled_first).astype(F32), (tokens - 64 < filled_second).astype(F32)
        )

    def prepare(j):
        start_first, start_second = meta[j, 0:1, :], meta[j, 1:2, :]
        filled_first, filled_second = meta[j, 2:3, :], meta[j, 3:4, :]
        cut = ((row_of >= 64) & (lane_of < 64)).astype(F32) * start_second
        seen = (lane_of <= row_of).astype(F32) * (1.0 - cut)
        mask[...] = seen * usable(lane_of, filled_first, filled_second)
        cut = ((lane_of >= 64) & (row_of < 64)).astype(F32) * start_second
        seen = (row_of <= lane_of).astype(F32) * (1.0 - cut)
        of_rows = usable(row_of, filled_first, filled_second)
        mask_t[...] = seen * of_rows
        kept = 1.0 - start_first
        bef[...] = jnp.where(row_of < 64, kept, kept * (1.0 - start_second)).astype(BF16)
        tail = jnp.where(row_of < 64, 1.0 - start_second, jnp.ones_like(start_second))
        trail[...] = (tail * of_rows).astype(BF16)
        return kept * (1.0 - start_second)

    @pl.when(jnp.logical_not(has_before))
    def _():
        states[0] = jnp.zeros_like(states[0])

    @pl.when(shift != 0)
    def _():
        states[shift] = jnp.zeros_like(states[0])

    @pl.when(section == 0)
    def _():
        pieces.wait(*rows_moves)

    @pl.when(section == 1)
    def _():
        forward_rows.wait_recv()
        pieces.start(*grad_moves)

    def first_norm(k):
        at = tile(k, 384)
        standard, _ = normalised(rows[at, :].astype(F32))
        normed[at, :] = (standard * first_gain[...].astype(F32) + first_shift[...].astype(F32)).astype(BF16)

    loop(2, first_norm)

    def project(k):
        at = tile(k, 256)
        proj[:, at] = (dot_nn(normed[...], qkv_w[:, at]) + qkv_b[:, at].astype(F32)).astype(BF16)

    weight(0).wait()
    loop(9, project)
    put(normed, 6)

    def features(p):
        low = low_lanes(6 * ROWS)
        for source, table, target in ((0, map_q, phi_q), (6, map_k, phi_k)):
            logits = dot_nn(proj[:, tile(source + p, 128)], table[p])
            for half in range(2):
                phi = half_softmax(logits[:, half * 128 : half * 128 + 128], low, ones[...])
                target[:, tile(2 * p + half, 128)] = phi.astype(BF16)

    loop(PAIRS, features)

    def attend(k):
        j = (shift + k) % 6

        @pl.when((j == 0) & has_before)
        def _():
            state_on.wait_recv()

        keep = prepare(j)
        at = tile(j, ROWS)

        def group(g):
            stores = []
            for p in [g * GROUP + q for q in range(GROUP)]:
                values = proj[at, tile(12 + p, 128)]
                results = []
                for half in range(2):
                    h = 2 * p + half
                    own = low if half == 0 else jnp.logical_not(low)
                    extended = jnp.where(own, values, jnp.ones_like(values))
                    queries, keys = phi_q[at, tile(h, 128)], phi_k[at, tile(h, 128)]
                    high, rest = high_low(dot_nt(queries, keys) * mask[...])
                    state = states[j, h]
                    state_high, state_low = high_low(state)
                    early = queries * bef[...]
                    results.append(
                        dot_nn(
                            jnp.concatenate([high, rest, early, early], 1),
                            jnp.concatenate([extended, extended, state_high, state_low], 0),
                        )
                    )
                    later = keep * state + dot_tn(keys * trail[...], extended)
                    stores.append((states, (j + 1, h), later))
                top = jnp.where(low, results[0], results[1])
                bottom = pltpu.roll(jnp.where(low, results[1], results[0]), 64, 1)
                share = top / bottom
                here = (at, tile(p, 128))
                stores += [(att_wide, here, share), (den, here, bottom), (att, here, share.astype(BF16))]
            for target, place, value in stores:
                target[place] = value

        loop(PAIRS // GROUP, group)

        @pl.when((j == 5) & has_after)
        def _():
            state_on.start()

    pieces.wait(*meta_moves)
    loop(6, attend)
    put(att, 5)

    def branch_out(k):
        at = tile(k, 256)
        total = dot_nn(att[...], out_w[:, at]) + out_b[:, at].astype(F32)
        res[:, at] = rows[:, at].astype(F32) + total

    weight(1).wait()
    loop(3, branch_out)
    put_done(normed, 6)

    def second_norm(k):
        at = tile(k, 384)
        standard, _ = normalised(res[at, :])
        normed[at, :] = (standard * second_gain[...].astype(F32) + second_shift[...].astype(F32)).astype(BF16)

    loop(2, second_norm)
    put(normed, 4)

    def feed(k):
        at = tile(k, 256)
        hidden = dot_nn(normed[...], up_w[:, at]) + up_b[:, at].astype(F32)
        square = hidden * hidden
        inner = hidden * (0.7978845608028654 + 0.0356774081363 * square)
        bent = jnp.tanh(inner)
        half = 0.5 * (1.0 + bent)
        act[:, at] = (hidden * half).astype(BF16)
        steep = 1.5957691216057308 + 0.2140644489 * square
        slope[:, at] = (half + hidden * half * (1.0 - half) * steep).astype(BF16)

    weight(2).wait()
    loop(12, feed)
    for n in range(4):
        put(act.at[:, pl.ds(n * WIDE, WIDE)], n)

    def settle(k):
        at = tile(k, 256)
        total = res[:, at] + dot_nn(act[...], down_w[:, at]) + down_b[:, at].astype(F32)
        branch[:, at] = total.astype(BF16)

    weight(3).wait()
    loop(3, settle)

    @pl.when(section == 0)
    def _():
        forward_rows.start()
        forward_rows.wait_send()
        backward_rows.wait_recv()

    @pl.when(section == 1)
    def _():
        pieces.wait(*grad_moves)
        copy = pltpu.make_async_copy(branch, ends, out_sem)
        copy.start()
        copy.wait()

    put(grad_in, 7)

    def column_sums(values):
        return jnp.sum(values.astype(F32), 0, keepdims=True)

    small[140:141, :] = column_sums(grad_in[...])

    def feed_back(k):
        at = tile(k, 256)
        grads = dot_nt(grad_in[...], down_w[at, :])
        grads = (grads * slope[:, at].astype(F32)).astype(BF16)
        slope[:, at] = grads

    loop(12, feed_back)
    for n in range(4):
        put(slope.at[:, pl.ds(n * WIDE, WIDE)], 8 + n)
        small[136 + n : 137 + n, :] = column_sums(slope[:, n * WIDE : n * WIDE + WIDE])

    def second_grad(k):
        at = tile(k, 256)
        grad_wide[:, at] = dot_nt(slope[...], up_w[at, :])

    loop(3, second_grad)

    def second_back(k):
        at = tile(k, 384)
        grads = grad_wide[at, :]
        standard, scale = normalised(res[at, :])
        small[134:135, :] += jnp.sum(grads * standard, 0, keepdims=True)
        small[135:136, :] += jnp.sum(grads, 0, keepdims=True)
        grads = norm_input_grad(grads, standard, scale, second_gain[...].astype(F32))
        grads = grad_in[at, :].astype(F32) + grads
        res[at, :] = grads
        rounded = grads.astype(BF16)
        branch[at, :] = rounded
        small[133:134, :] += column_sums(rounded)

    loop(2, second_back)
    put(branch, 12)

    def attended_grad(k):
        at = tile(k, 256)
        grad_wide[:, at] = dot_nt(branch[...], out_w[at, :])

    loop(3, attended_grad)
    for n in range(4):
        put_done(act.at[:, pl.ds(n * WIDE, WIDE)], n)

    put_done(att, 5)
    back_state[...] = jnp.zeros_like(back_state)

    def attend_back(k):
        j = (shift + 5 - k) % 6

        @pl.when(j == 5)
        def _():
            @pl.when(has_after)
            def _():
                state_back.wait_recv()
                back_state[...] = back_in[...]

            @pl.when(jnp.logical_not(has_after))
            def _():
                back_state[...] = jnp.zeros_like(back_state)

        keep = prepare(j)
        at = tile(j, ROWS)

        def group(g):
            stores = []
            for p in [g * GROUP_BACK + q for q in range(GROUP_BACK)]:
                values = proj[at, tile(12 + p, 128)]
                grads = (grad_wide[at, tile(p, 128)] / den[at, tile(p, 128)]).astype(BF16)
                sums = -half_sums(grads.astype(F32) * att_wide[at, tile(p, 128)], low)
                other_sums = pltpu.roll(sums, 64, 1)
                lanes = lax.broadcasted_iota(jnp.int32, (ROWS, 128), 1) % 64
                one = other_sums.astype(BF16).astype(F32)
                two = (other_sums - one).astype(BF16).astype(F32)
                three = other_sums - one - two
                spread = jnp.where(lanes == 0, one, jnp.where(lanes == 1, two, jnp.where(lanes == 2, three, 0.0)))
                spread = spread.astype(BF16)
                value_grads, query_grads, key_grads = [], [], []
                for half in range(2):
                    h = 2 * p + half
                    own = low if half == 0 else jnp.logical_not(low)
                    extended = jnp.where(own, values, jnp.ones_like(values))
                    grads_ext = jnp.where(own, grads, spread)
                    queries, keys = phi_q[at, tile(h, 128)], phi_k[at, tile(h, 128)]
                    high, rest = high_low(dot_nt(grads_ext, extended) * mask[...])
                    state_high, state_low = high_low(states[j, h])
                    query_grad = dot_nn(
                        jnp.concatenate([high, rest], 1), jnp.concatenate([keys, keys], 0)
                    )
                    query_grad += bef[...].astype(F32) * dot_nt(
                        jnp.concatenate([grads_ext, grads_ext], 1),
                        jnp.concatenate([state_high, state_low], 1),
                    )
                    high, rest = high_low(dot_nt(extended, grads_ext) * mask_t[...])
                    later = back_state[h]
                    later_high, later_low = high_low(later)
                    key_grad = dot_nn(
                        jnp.concatenate([high, rest], 1), jnp.concatenate([queries, queries], 0)
                    )
                    key_grad += trail[...].astype(F32) * dot_nt(
                        jnp.concatenate([extended, extended], 1),
                        jnp.concatenate([later_high, later_low], 1),
                    )
                    scores_t = (dot_nt(keys, queries) * mask_t[...]).astype(BF16)
                    value_grads.append(
                        dot_nn(
                            jnp.concatenate([scores_t, keys * trail[...]], 1),
                            jnp.concatenate([grads_ext, later_high], 0),
                        )
                    )
                    stores.append((back_state, h, keep * later + dot_tn(queries * bef[...], grads_ext)))
                    for phi, grad, kept in ((queries, query_grad, query_grads), (keys, key_grad, key_grads)):
                        phi = phi.astype(F32)
                        kept.append(phi * (grad - half_sums(phi * grad, low)))
                value_grad = jnp.where(low, value_grads[0], value_grads[1]).astype(BF16)
                stores.append((act, (at, tile(12 + p, 128)), value_grad))
                for kept, target, first in ((query_grads, act, 18), (key_grads, att, 0)):
                    left = kept[0] - pltpu.roll(kept[0], 64, 1)
                    right = pltpu.roll(kept[1], 64, 1) - kept[1]
                    both = jnp.where(low, left, right).astype(BF16)
                    stores.append((target, (at, tile(first + p, 128)), both))
            for target, place, value in stores:
                target[place] = value

        loop(PAIRS // GROUP_BACK, group)

        @pl.when((j == 0) & has_before)
        def _():
            back_out[...] = back_state[...]
            state_back.start()

    loop(6, attend_back)

    def maps_back(p):
        lanes = tile(p, 128)
        first = lax.broadcasted_iota(jnp.int32, (64, 128), 1) < 64
        for offset, target, source, table, at in ((0, act, 18, pair_q, 0), (6, att, 0, pair_k, 64)):
            logit_grads = target[:, tile(source + p, 128)]
            act[:, tile(offset + p, 128)] = dot_nt(logit_grads, table[p]).astype(BF16)
            product = dot_tn(proj[:, tile(offset + p, 128)], logit_grads)
            small[at : at + 64, lanes] = jnp.where(first, product[:64], product[64:])

    loop(PAIRS, maps_back)
    for n in range(3):
        put(act.at[:, pl.ds(n * WIDE, WIDE)], 13 + n)
        small[130 + n : 131 + n, :] = column_sums(act[:, n * WIDE : n * WIDE + WIDE])

    def first_grad(k):
        at = tile(k, 256)
        grad_wide[:, at] = dot_nt(act[:, : 3 * WIDE], qkv_w[at, :])

    loop(3, first_grad)

    def first_back(k):
        at = tile(k, 384)
        grads = grad_wide[at, :]
        standard, scale = normalised(rows[at, :].astype(F32))
        small[128:129, :] += jnp.sum(grads * standard, 0, keepdims=True)
        small[129:130, :] += jnp.sum(grads, 0, keepdims=True)
        grads = norm_input_grad(grads, standard, scale, first_gain[...].astype(F32))
        rows[at, :] = (res[at, :] + grads).astype(BF16)

    loop(2, first_back)

    @pl.when(section == 1)
    def _():
        backward_rows.start()
        backward_rows.wait_send()

    @pl.when(section == 0)
    def _():
        copy = pltpu.make_async_copy(rows, ends, out_sem)
        copy.start()
        copy.wait()

    put_done(normed, 4)
    put_done(grad_in, 7)
    put_done(branch, 12)
    for n in range(4):
        put_done(slope.at[:, pl.ds(n * WIDE, WIDE)], 8 + n)
    for n in range(3):
        put_done(act.at[:, pl.ds(n * WIDE, WIDE)], 13 + n)

    @pl.when(has_after)
    def _():
        state_on.wait_send()

    @pl.when(has_before)
    def _():
        state_back.wait_send()


def layers(ends_in, begins, filled, weights, mesh):
    tokens = 6 * ROWS
    any_space = pl.BlockSpec(memory_space=pl.ANY)
    in_vmem = pl.BlockSpec(memory_space=pltpu.VMEM)
    large = (2, 6, 10, 12)
    return pl.pallas_call(
        functools.partial(layers_kernel, mesh.shape["ctx"]),
        out_shape=(
            jax.ShapeDtypeStruct((16, tokens, WIDE), BF16),
            jax.ShapeDtypeStruct((tokens, WIDE), BF16),
            jax.ShapeDtypeStruct((256, WIDE), F32),
        ),
        in_specs=[any_space] + [in_vmem] * 2 + [any_space if n in large else in_vmem for n in range(14)],
        out_specs=(any_space, any_space, in_vmem),
        scratch_shapes=[
            pltpu.VMEM((WIDE, 3 * WIDE), BF16),
            pltpu.VMEM((WIDE, WIDE), BF16),
            pltpu.VMEM((WIDE, 4 * WIDE), BF16),
            pltpu.VMEM((4 * WIDE, WIDE), BF16),
            pltpu.VMEM((PAIRS, 128, 256), BF16),
            pltpu.VMEM((PAIRS, 128, 256), BF16),
            pltpu.VMEM((PAIRS, 128, 128), BF16),
            pltpu.VMEM((PAIRS, 128, 128), BF16),
            pltpu.VMEM((6, 8, 128), F32),
            pltpu.VMEM((6, 8, 128), F32),
            pltpu.VMEM((tokens, WIDE), BF16),
            pltpu.VMEM((tokens, WIDE), BF16),
            pltpu.VMEM((tokens, WIDE), BF16),
            pltpu.VMEM((tokens, 3 * WIDE), BF16),
            pltpu.VMEM((tokens, 2 * WIDE), BF16),
            pltpu.VMEM((tokens, 2 * WIDE), BF16),
            pltpu.VMEM((tokens, WIDE), BF16),
            pltpu.VMEM((tokens, WIDE), F32),
            pltpu.VMEM((tokens, WIDE), F32),
            pltpu.VMEM((tokens, WIDE), F32),
            pltpu.VMEM((tokens, 4 * WIDE), BF16),
            pltpu.VMEM((tokens, 4 * WIDE), BF16),
            pltpu.VMEM((7, HEADS, 128, 128), F32),
            pltpu.VMEM((HEADS, 128, 128), F32),
            pltpu.VMEM((HEADS, 128, 128), F32),
            pltpu.VMEM((HEADS, 128, 128), F32),
            pltpu.VMEM((tokens, WIDE), F32),
            pltpu.VMEM((tokens, WIDE), BF16),
            pltpu.VMEM((128, 128), BF16),
            pltpu.VMEM((128, 128), F32),
            pltpu.VMEM((128, 128), F32),
            pltpu.VMEM((128, 128), BF16),
            pltpu.VMEM((128, 128), BF16),
            pltpu.SemaphoreType.DMA((16,)),
            pltpu.SemaphoreType.DMA,
            pltpu.SemaphoreType.DMA((4, 2)),
            pltpu.SemaphoreType.DMA((4,)),
            pltpu.SemaphoreType.DMA((2, 3, 6)),
        ],
        compiler_params=pltpu.CompilerParams(
            collective_id=1, has_side_effects=True, vmem_limit_bytes=60 * 1024 * 1024
        ),
    )(ends_in, begins, filled, *weights)


def body(mesh, ends_in, begins, filled, *weights):
    x, ends, small = layers(ends_in, begins, filled, weights, mesh)
    sums, small, ends = reduced(x, small, ends, mesh)
    return finished(sums, small, ends, weights)


def solution(mesh):
    placed = (
        P("section", None, ("dp", "ctx"), None),
        P(None, ("dp", "ctx")),
        P(None, ("dp", "ctx")),
        P("section", None),
        P("section", None),
        P("section", None, None),
        P("section", None),
        P("section", None, None),
        P("section", None, None),
        P("section", None, None),
        P("section", None),
        P("section", None),
        P("section", None),
        P("section", None, None),
        P("section", None),
        P("section", None, None),
        P("section", None),
    )
    return jax.shard_map(
        functools.partial(body, mesh),
        mesh=mesh,
        in_specs=placed,
        out_specs=(
            P("section", None, ("dp", "ctx"), None),
            P("section", None),
            P("section", None),
            P("section", None, None),
            P("section", None),
            P("section", None, None),
            P("section", None, None),
            P("section", None, None),
            P("section", None),
            P("section", None),
            P("section", None),
            P("section", None, None),
            P("section", None),
            P("section", None, None),
            P("section", None),
        ),
        check_vma=False,
    )
```

time: 519 us -> 405 us (0.78)
  Pallas kernels: 483 us -> 401 us
  local copies, waits for them, and re-layouts: 31.7 us -> 2.7 us
    pallas_call x1, Pallas kernels: 288 us -> 209 us  [layers(): pl.pallas_call(functools.partial(layers_kernel, mesh.shape['ctx']), out_s...]
    unnamed x32 -> x2, local copies, waits for them, and re-layouts: 26.1 us -> 2.7 us
    pallas_call x3 -> x2, Pallas kernels: 195 us -> 192 us  [the longest x1 175 us: reduced(): pl.pallas_call(functools.partial(reduce_kernel, orders, mesh.shape['ctx']...]
where the time goes in v3:
time: 405 us; the launch traced here: 404 us
  Pallas kernels  401 us (99%)
    pallas_call x1, Pallas kernels, layers(): pl.pallas_call(functools.partial(layers_kernel, mesh.shape['ctx']), out_s...  209 us
    pallas_call x1, Pallas kernels, reduced(): pl.pallas_call(functools.partial(reduce_kernel, orders, mesh.shape['ctx']...  175 us
    pallas_call x1, Pallas kernels, finished(): pl.pallas_call(finish_kernel, out_shape=tuple(shapes), in_specs=[any_spac...  16.9 us

profile of v3, /device:TPU:0, one launch (start us, length us, event | category | flops | bytes accessed | tf_op | source)
XLA Modules:
  0.0 404.4 jit_solution(5612891161763350590)
XLA Ops:
  0.6 1.4 copy.32.refs_1_
  2.0 1.4 copy.33.refs_2_
  3.3 208.9 %shard_map.280 = (bf16[16,768,768]{2,1,0:T(8,128)(2,1)}, bf16[768,768]{1,0:T(8,128)(2,1)}, f32[256,768]{1,0:T(8,128)}) custom-call(bf16[1,6,128,768]{3,2,1,0:T(8,128)(2,1)} %refs_0_.1, s32[6,2]{1,0:T(8,128)} %copy.32.refs_1_, s32[6,2]{1,0:T(8,128)} %copy.33.refs_2_, bf16[1,768]{1,0:T(2,128)(2,1)} %refs_3_.1, bf16[1,768]{1,0:T(2,128)(2,1)} %refs_4_.1, ...), custom_call_target="tpu_custom_call" | custom-call | tf_op jit(solution)/shard_map/pallas_call | solution.py:909
  212.2 175.1 %shard_map.281 = (bf16[12,768,768]{2,1,0:T(8,128)(2,1)}, bf16[256,768]{1,0:T(8,128)(2,1)}, bf16[6,128,768]{2,1,0:T(8,128)(2,1)}) custom-call(bf16[16,768,768]{2,1,0:T(8,128)(2,1)} %get-tuple-element.21.x_ref, f32[256,768]{1,0:T(8,128)} %get-tuple-element.22.small_ref, bf16[768,768]{1,0:T(8,128)(2,1)} %get-tuple-element.23.ends), custom_call_target="tpu_custom_call" | custom-call | tf_op jit(solution)/shard_map/pallas_call | solution.py:292
  387.4 16.9 %shard_map.282 = (bf16[1,6,128,768]{3,2,1,0:T(8,128)(2,1)}, f32[1,768]{1,0:T(1,128)}, f32[1,768]{1,0:T(1,128)}, f32[1,768,2304]{2,1,0:T(8,128)}, f32[1,2304]{1,0...) custom-call(bf16[12,768,768]{2,1,0:T(8,128)(2,1)} %get-tuple-element, ...), custom_call_target="tpu_custom_call" | custom-call | tf_op jit(solution)/shard_map/pallas_call | solution.py:382

commit v4 on v3

--- a/solution.py
+++ b/solution.py
@@ -224,6 +224,7 @@
 
     for part in range(2):
         small_copy(part, 0).start()
+    section = lax.axis_index("section")
     pieces = Pieces(ctx_size, False)
     given = (lambda k: ends.at[block_rows(k), :], lambda k: ends_out.at[k], moves)
 
@@ -243,7 +244,7 @@
             for part in range(2):
                 big_copy(t, part, 0).start()
 
-        @pl.when(t == chunks)
+        @pl.when((t == chunks) & (section == 0))
         def _():
             pieces.start(*given)
 
@@ -275,7 +276,16 @@
 
     lax.fori_loop(0, chunks + steps, tick, 0)
     small_out[...] = little_whole[...]
-    pieces.wait(*given)
+
+    @pl.when(section == 0)
+    def _():
+        pieces.wait(*given)
+
+    @pl.when(section == 1)
+    def _():
+        for k in range(6):
+            ends_out[k] = ends[block_rows(k), :]
+
     pltpu.make_async_copy(big_whole, sums, store).wait()
 
 
@@ -460,12 +470,12 @@
 
 def layers_kernel(ctx_size, *refs):
     (
-        x_in, begins, filled, first_gain, first_shift, qkv_given, qkv_b, map_q_given, map_k_given,
+        x_in, flags, first_gain, first_shift, qkv_given, qkv_b, map_q_given, map_k_given,
         out_given, out_b, second_gain, second_shift, up_given, up_b, down_given, down_b,
         x_out, ends, small,
         qkv_w, out_w, up_w, down_w, map_q, map_k, pair_q, pair_k, meta_own, meta,
         rows, grad_in, normed, proj, phi_q, phi_k, att, att_wide, den, res, act, slope,
-        states, back_state, back_in, back_out, grad_wide, branch,
+        states, pack_in, pack_out, back_state, back_in, back_out, grad_wide, branch,
         ones, mask, mask_t, bef, trail, x_sem, out_sem, remote, weight_sem, moves,
     ) = refs
     section, me = lax.axis_index("section"), lax.axis_index("ctx")
@@ -489,23 +499,30 @@
             device_id_type=MESH,
         )
 
-    forward_rows = remote_copy(branch, rows, 0, other)
-    backward_rows = remote_copy(rows, grad_in, 1, other)
-    state_on = remote_copy(states.at[6], states.at[0], 2, {"ctx": me + 1})
-    state_back = remote_copy(back_out, back_in, 3, {"ctx": me - 1})
+    def forward_rows(k):
+        at = tile(k, 384)
+        return remote_copy(branch.at[at, :], rows.at[at, :], k, other)
+
+    def backward_rows(k):
+        at = tile(k, 384)
+        return remote_copy(rows.at[at, :], grad_in.at[at, :], 2 + k, other)
+
+    state_on = remote_copy(pack_out, pack_in, 4, {"ctx": me + 1})
+    state_back = remote_copy(back_out, back_in, 5, {"ctx": me - 1})
     pieces = Pieces(ctx_size, True)
     rows_moves = (lambda k: x_in.at[0, k], lambda k: rows.at[block_rows(k), :], moves.at[0])
     grad_moves = (lambda k: x_in.at[0, k], lambda k: grad_in.at[block_rows(k), :], moves.at[0])
+    back_pieces = Pieces(ctx_size, False)
+    ends_moves = (lambda k: branch.at[block_rows(k), :], lambda k: ends.at[block_rows(k), :], moves.at[2])
     meta_moves = (lambda k: meta_own.at[k], lambda k: meta.at[k], moves.at[1])
 
     barrier = pltpu.get_barrier_semaphore()
     greeted = greet_ctx(barrier, ctx_size)
     pl.semaphore_signal(barrier, inc=1, device_id=other, device_id_type=MESH)
     for k in range(6):
-        for n, source in ((0, begins), (2, filled)):
-            for half in range(2):
-                value = source[k : k + 1, half : half + 1].astype(F32)
-                meta_own[k, n + half : n + half + 1, :] = jnp.broadcast_to(value, (1, 128))
+        for n in range(4):
+            value = flags[k : k + 1, n : n + 1].astype(F32)
+            meta_own[k, n : n + 1, :] = jnp.broadcast_to(value, (1, 128))
     pl.semaphore_wait(barrier, greeted + 1)
 
     @pl.when(section == 0)
@@ -559,6 +576,25 @@
         trail[...] = (tail * of_rows).astype(BF16)
         return kept * (1.0 - start_second)
 
+    def pack(source, target):
+        sums = jnp.zeros((128, 128), F32)
+        for p in range(PAIRS):
+            first, second = source(2 * p), source(2 * p + 1)
+            target[p] = jnp.where(low, first, second)
+            first = jnp.sum(jnp.where(low, 0.0, first), -1, keepdims=True)
+            second = jnp.sum(jnp.where(low, second, 0.0), -1, keepdims=True)
+            sums = jnp.where(lane_of == 2 * p, first, jnp.where(lane_of == 2 * p + 1, second, sums))
+        target[PAIRS] = sums
+
+    def unpack(source, store, share):
+        sums = source[PAIRS]
+        for p in range(PAIRS):
+            both = source[p]
+            first = jnp.sum(jnp.where(lane_of == 2 * p, sums, 0.0), -1, keepdims=True)
+            second = jnp.sum(jnp.where(lane_of == 2 * p + 1, sums, 0.0), -1, keepdims=True)
+            store(2 * p, jnp.where(low, both, first * share))
+            store(2 * p + 1, jnp.where(low, second * share, both))
+
     @pl.when(jnp.logical_not(has_before))
     def _():
         states[0] = jnp.zeros_like(states[0])
@@ -573,10 +609,14 @@
 
     @pl.when(section == 1)
     def _():
-        forward_rows.wait_recv()
+        forward_rows(0).wait_recv()
         pieces.start(*grad_moves)
 
     def first_norm(k):
+        @pl.when((section == 1) & (k == 1))
+        def _():
+            forward_rows(1).wait_recv()
+
         at = tile(k, 384)
         standard, _ = normalised(rows[at, :].astype(F32))
         normed[at, :] = (standard * first_gain[...].astype(F32) + first_shift[...].astype(F32)).astype(BF16)
@@ -584,11 +624,11 @@
     loop(2, first_norm)
 
     def project(k):
-        at = tile(k, 256)
+        at = tile(k, 768)
         proj[:, at] = (dot_nn(normed[...], qkv_w[:, at]) + qkv_b[:, at].astype(F32)).astype(BF16)
 
     weight(0).wait()
-    loop(9, project)
+    loop(3, project)
     put(normed, 6)
 
     def features(p):
@@ -607,6 +647,11 @@
         @pl.when((j == 0) & has_before)
         def _():
             state_on.wait_recv()
+
+            def keep_state(h, value):
+                states[0, h] = value
+
+            unpack(pack_in, keep_state, 0.015625)
 
         keep = prepare(j)
         at = tile(j, ROWS)
@@ -645,6 +690,7 @@
 
         @pl.when((j == 5) & has_after)
         def _():
+            pack(lambda h: states[6, h], pack_out)
             state_on.start()
 
     pieces.wait(*meta_moves)
@@ -685,25 +731,28 @@
         put(act.at[:, pl.ds(n * WIDE, WIDE)], n)
 
     def settle(k):
-        at = tile(k, 256)
-        total = res[:, at] + dot_nn(act[...], down_w[:, at]) + down_b[:, at].astype(F32)
-        branch[:, at] = total.astype(BF16)
+        at = tile(k, 384)
+        total = res[at, :] + dot_nn(act[at, :], down_w[...]) + down_b[...].astype(F32)
+        branch[at, :] = total.astype(BF16)
+
+        @pl.when(section == 0)
+        def _():
+            forward_rows(k).start()
 
     weight(3).wait()
-    loop(3, settle)
+    loop(2, settle)
 
     @pl.when(section == 0)
     def _():
-        forward_rows.start()
-        forward_rows.wait_send()
-        backward_rows.wait_recv()
+        for k in range(2):
+            forward_rows(k).wait_send()
+        for k in range(2):
+            backward_rows(k).wait_recv()
 
     @pl.when(section == 1)
     def _():
+        back_pieces.start(*ends_moves)
         pieces.wait(*grad_moves)
-        copy = pltpu.make_async_copy(branch, ends, out_sem)
-        copy.start()
-        copy.wait()
 
     put(grad_in, 7)
 
@@ -713,12 +762,12 @@
     small[140:141, :] = column_sums(grad_in[...])
 
     def feed_back(k):
-        at = tile(k, 256)
+        at = tile(k, 512)
         grads = dot_nt(grad_in[...], down_w[at, :])
         grads = (grads * slope[:, at].astype(F32)).astype(BF16)
         slope[:, at] = grads
 
-    loop(12, feed_back)
+    loop(6, feed_back)
     for n in range(4):
         put(slope.at[:, pl.ds(n * WIDE, WIDE)], 8 + n)
         small[136 + n : 137 + n, :] = column_sums(slope[:, n * WIDE : n * WIDE + WIDE])
@@ -742,6 +791,10 @@
         branch[at, :] = rounded
         small[133:134, :] += column_sums(rounded)
 
+    @pl.when(section == 1)
+    def _():
+        back_pieces.wait(*ends_moves)
+
     loop(2, second_back)
     put(branch, 12)
 
@@ -764,7 +817,12 @@
             @pl.when(has_after)
             def _():
                 state_back.wait_recv()
-                back_state[...] = back_in[...]
+
+                def keep_state(h, value):
+                    back_state[h] = value
+
+                first_lane = ((lane_of == 0) | (lane_of == 64)).astype(F32)
+                unpack(back_in, keep_state, first_lane)
 
             @pl.when(jnp.logical_not(has_after))
             def _():
@@ -837,7 +895,7 @@
 
         @pl.when((j == 0) & has_before)
         def _():
-            back_out[...] = back_state[...]
+            pack(lambda h: back_state[h], back_out)
             state_back.start()
 
     loop(6, attend_back)
@@ -871,12 +929,11 @@
         grads = norm_input_grad(grads, standard, scale, first_gain[...].astype(F32))
         rows[at, :] = (res[at, :] + grads).astype(BF16)
 
+        @pl.when(section == 1)
+        def _():
+            backward_rows(k).start()
+
     loop(2, first_back)
-
-    @pl.when(section == 1)
-    def _():
-        backward_rows.start()
-        backward_rows.wait_send()
 
     @pl.when(section == 0)
     def _():
@@ -891,6 +948,11 @@
         put_done(slope.at[:, pl.ds(n * WIDE, WIDE)], 8 + n)
     for n in range(3):
         put_done(act.at[:, pl.ds(n * WIDE, WIDE)], 13 + n)
+
+    @pl.when(section == 1)
+    def _():
+        for k in range(2):
+            backward_rows(k).wait_send()
 
     @pl.when(has_after)
     def _():
@@ -913,7 +975,7 @@
             jax.ShapeDtypeStruct((tokens, WIDE), BF16),
             jax.ShapeDtypeStruct((256, WIDE), F32),
         ),
-        in_specs=[any_space] + [in_vmem] * 2 + [any_space if n in large else in_vmem for n in range(14)],
+        in_specs=[any_space, in_vmem] + [any_space if n in large else in_vmem for n in range(14)],
         out_specs=(any_space, any_space, in_vmem),
         scratch_shapes=[
             pltpu.VMEM((WIDE, 3 * WIDE), BF16),
@@ -939,9 +1001,11 @@
             pltpu.VMEM((tokens, 4 * WIDE), BF16),
             pltpu.VMEM((tokens, 4 * WIDE), BF16),
             pltpu.VMEM((7, HEADS, 128, 128), F32),
+            pltpu.VMEM((PAIRS + 1, 128, 128), F32),
+            pltpu.VMEM((PAIRS + 1, 128, 128), F32),
             pltpu.VMEM((HEADS, 128, 128), F32),
-            pltpu.VMEM((HEADS, 128, 128), F32),
-            pltpu.VMEM((HEADS, 128, 128), F32),
+            pltpu.VMEM((PAIRS + 1, 128, 128), F32),
+            pltpu.VMEM((PAIRS + 1, 128, 128), F32),
             pltpu.VMEM((tokens, WIDE), F32),
             pltpu.VMEM((tokens, WIDE), BF16),
             pltpu.VMEM((128, 128), BF16),
@@ -951,14 +1015,14 @@
             pltpu.VMEM((128, 128), BF16),
             pltpu.SemaphoreType.DMA((16,)),
             pltpu.SemaphoreType.DMA,
-            pltpu.SemaphoreType.DMA((4, 2)),
+            pltpu.SemaphoreType.DMA((6, 2)),
             pltpu.SemaphoreType.DMA((4,)),
-            pltpu.SemaphoreType.DMA((2, 3, 6)),
+            pltpu.SemaphoreType.DMA((3, 3, 6)),
         ],
         compiler_params=pltpu.CompilerParams(
             collective_id=1, has_side_effects=True, vmem_limit_bytes=60 * 1024 * 1024
         ),
-    )(ends_in, begins, filled, *weights)
+    )(ends_in, jnp.concatenate([begins, filled], 1), *weights)
 
 
 def body(mesh, ends_in, begins, filled, *weights):

time: 405 us -> 390 us (0.963)
  Pallas kernels: 401 us -> 386 us
    pallas_call x1, Pallas kernels: 209 us -> 192 us  [layers(): pl.pallas_call(functools.partial(layers_kernel, mesh.shape['ctx']), out_s...]
where the time goes in v4:
time: 390 us; the launch traced here: 389 us
  Pallas kernels  386 us (99%)
    pallas_call x1, Pallas kernels, layers(): pl.pallas_call(functools.partial(layers_kernel, mesh.shape['ctx']), out_s...  192 us
    pallas_call x1, Pallas kernels, reduced(): pl.pallas_call(functools.partial(reduce_kernel, orders, mesh.shape['ctx']...  177 us
    pallas_call x1, Pallas kernels, finished(): pl.pallas_call(finish_kernel, out_shape=tuple(shapes), in_specs=[any_spac...  16.9 us

profile of v4, /device:TPU:0, one launch (start us, length us, event | category | flops | bytes accessed | tf_op | source)
XLA Modules:
  0.0 389.3 jit_solution(1701088350443154921)
XLA Ops:
  0.6 0.8 copy.32
  1.4 0.8 copy.33
  2.2 0.7 pad_add_fusion.refs_1_
  2.8 192.1 %shard_map.280 = (bf16[16,768,768]{2,1,0:T(8,128)(2,1)}, bf16[768,768]{1,0:T(8,128)(2,1)}, f32[256,768]{1,0:T(8,128)}) custom-call(bf16[1,6,128,768]{3,2,1,0:T(8,128)(2,1)} %refs_0_.1, s32[6,4]{1,0:T(8,128)} %pad_add_fusion.refs_1_, bf16[1,768]{1,0:T(2,128)(2,1)} %refs_2_.1, bf16[1,768]{1,0:T(2,128)(2,1)} %refs_3_.1, bf16[1,768,2304]{2,1,0:T(8,128)(2,1)} %refs_4_.1, ...), custom_call_target="tpu_custom_call" | custom-call | tf_op jit(solution)/shard_map/pallas_call | solution.py:971
  194.9 177.3 %shard_map.281 = (bf16[12,768,768]{2,1,0:T(8,128)(2,1)}, bf16[256,768]{1,0:T(8,128)(2,1)}, bf16[6,128,768]{2,1,0:T(8,128)(2,1)}) custom-call(bf16[16,768,768]{2,1,0:T(8,128)(2,1)} %get-tuple-element.21.x_ref, f32[256,768]{1,0:T(8,128)} %get-tuple-element.22.small_ref, bf16[768,768]{1,0:T(8,128)(2,1)} %get-tuple-element.23.ends), custom_call_target="tpu_custom_call" | custom-call | tf_op jit(solution)/shard_map/pallas_call | solution.py:302
  372.2 16.9 %shard_map.282 = (bf16[1,6,128,768]{3,2,1,0:T(8,128)(2,1)}, f32[1,768]{1,0:T(1,128)}, f32[1,768]{1,0:T(1,128)}, f32[1,768,2304]{2,1,0:T(8,128)}, f32[1,2304]{1,0...) custom-call(bf16[12,768,768]{2,1,0:T(8,128)(2,1)} %get-tuple-element, ...), custom_call_target="tpu_custom_call" | custom-call | tf_op jit(solution)/shard_map/pallas_call | solution.py:392

commit v5 on v4

--- a/solution.py
+++ b/solution.py
@@ -475,7 +475,7 @@
         x_out, ends, small,
         qkv_w, out_w, up_w, down_w, map_q, map_k, pair_q, pair_k, meta_own, meta,
         rows, grad_in, normed, proj, phi_q, phi_k, att, att_wide, den, res, act, slope,
-        states, pack_in, pack_out, back_state, back_in, back_out, grad_wide, branch,
+        states, pack_in, pack_out, back_state, back_in, grad_wide, branch, branch_grad,
         ones, mask, mask_t, bef, trail, x_sem, out_sem, remote, weight_sem, moves,
     ) = refs
     section, me = lax.axis_index("section"), lax.axis_index("ctx")
@@ -508,7 +508,7 @@
         return remote_copy(rows.at[at, :], grad_in.at[at, :], 2 + k, other)
 
     state_on = remote_copy(pack_out, pack_in, 4, {"ctx": me + 1})
-    state_back = remote_copy(back_out, back_in, 5, {"ctx": me - 1})
+    state_back = remote_copy(pack_out, back_in, 5, {"ctx": me - 1})
     pieces = Pieces(ctx_size, True)
     rows_moves = (lambda k: x_in.at[0, k], lambda k: rows.at[block_rows(k), :], moves.at[0])
     grad_moves = (lambda k: x_in.at[0, k], lambda k: grad_in.at[block_rows(k), :], moves.at[0])
@@ -788,25 +788,25 @@
         grads = grad_in[at, :].astype(F32) + grads
         res[at, :] = grads
         rounded = grads.astype(BF16)
-        branch[at, :] = rounded
+        branch_grad[at, :] = rounded
         small[133:134, :] += column_sums(rounded)
 
-    @pl.when(section == 1)
-    def _():
-        back_pieces.wait(*ends_moves)
-
     loop(2, second_back)
-    put(branch, 12)
+    put(branch_grad, 12)
 
     def attended_grad(k):
         at = tile(k, 256)
-        grad_wide[:, at] = dot_nt(branch[...], out_w[at, :])
+        grad_wide[:, at] = dot_nt(branch_grad[...], out_w[at, :])
 
     loop(3, attended_grad)
     for n in range(4):
         put_done(act.at[:, pl.ds(n * WIDE, WIDE)], n)
 
     put_done(att, 5)
+    @pl.when(has_after)
+    def _():
+        state_on.wait_send()
+
     back_state[...] = jnp.zeros_like(back_state)
 
     def attend_back(k):
@@ -895,7 +895,7 @@
 
         @pl.when((j == 0) & has_before)
         def _():
-            pack(lambda h: back_state[h], back_out)
+            pack(lambda h: back_state[h], pack_out)
             state_back.start()
 
     loop(6, attend_back)
@@ -943,7 +943,7 @@
 
     put_done(normed, 4)
     put_done(grad_in, 7)
-    put_done(branch, 12)
+    put_done(branch_grad, 12)
     for n in range(4):
         put_done(slope.at[:, pl.ds(n * WIDE, WIDE)], 8 + n)
     for n in range(3):
@@ -951,12 +951,9 @@
 
     @pl.when(section == 1)
     def _():
+        back_pieces.wait(*ends_moves)
         for k in range(2):
             backward_rows(k).wait_send()
-
-    @pl.when(has_after)
-    def _():
-        state_on.wait_send()
 
     @pl.when(has_before)
     def _():
@@ -1005,8 +1002,8 @@
             pltpu.VMEM((PAIRS + 1, 128, 128), F32),
             pltpu.VMEM((HEADS, 128, 128), F32),
             pltpu.VMEM((PAIRS + 1, 128, 128), F32),
-            pltpu.VMEM((PAIRS + 1, 128, 128), F32),
             pltpu.VMEM((tokens, WIDE), F32),
+            pltpu.VMEM((tokens, WIDE), BF16),
             pltpu.VMEM((tokens, WIDE), BF16),
             pltpu.VMEM((128, 128), BF16),
             pltpu.VMEM((128, 128), F32),

time: 390 us -> 390 us (level)
  no operation moved by 1% of the time
where the time goes in v5:
time: 390 us; the launch traced here: 389 us
  Pallas kernels  386 us (99%)
    pallas_call x1, Pallas kernels, layers(): pl.pallas_call(functools.partial(layers_kernel, mesh.shape['ctx']), out_s...  192 us
    pallas_call x1, Pallas kernels, reduced(): pl.pallas_call(functools.partial(reduce_kernel, orders, mesh.shape['ctx']...  177 us
    pallas_call x1, Pallas kernels, finished(): pl.pallas_call(finish_kernel, out_shape=tuple(shapes), in_specs=[any_spac...  16.9 us

profile of v5, /device:TPU:0, one launch (start us, length us, event | category | flops | bytes accessed | tf_op | source)
XLA Modules:
  0.0 389.3 jit_solution(8841769019115490767)
XLA Ops:
  0.6 0.8 copy.32
  1.4 0.8 copy.33
  2.2 0.7 pad_add_fusion.refs_1_
  2.8 192.0 %shard_map.280 = (bf16[16,768,768]{2,1,0:T(8,128)(2,1)}, bf16[768,768]{1,0:T(8,128)(2,1)}, f32[256,768]{1,0:T(8,128)}) custom-call(bf16[1,6,128,768]{3,2,1,0:T(8,128)(2,1)} %refs_0_.1, s32[6,4]{1,0:T(8,128)} %pad_add_fusion.refs_1_, bf16[1,768]{1,0:T(2,128)(2,1)} %refs_2_.1, bf16[1,768]{1,0:T(2,128)(2,1)} %refs_3_.1, bf16[1,768,2304]{2,1,0:T(8,128)(2,1)} %refs_4_.1, ...), custom_call_target="tpu_custom_call" | custom-call | tf_op jit(solution)/shard_map/pallas_call | solution.py:968
  194.8 177.3 %shard_map.281 = (bf16[12,768,768]{2,1,0:T(8,128)(2,1)}, bf16[256,768]{1,0:T(8,128)(2,1)}, bf16[6,128,768]{2,1,0:T(8,128)(2,1)}) custom-call(bf16[16,768,768]{2,1,0:T(8,128)(2,1)} %get-tuple-element.21.x_ref, f32[256,768]{1,0:T(8,128)} %get-tuple-element.22.small_ref, bf16[768,768]{1,0:T(8,128)(2,1)} %get-tuple-element.23.ends), custom_call_target="tpu_custom_call" | custom-call | tf_op jit(solution)/shard_map/pallas_call | solution.py:302
  372.2 16.9 %shard_map.282 = (bf16[1,6,128,768]{3,2,1,0:T(8,128)(2,1)}, f32[1,768]{1,0:T(1,128)}, f32[1,768]{1,0:T(1,128)}, f32[1,768,2304]{2,1,0:T(8,128)}, f32[1,2304]{1,0...) custom-call(bf16[12,768,768]{2,1,0:T(8,128)(2,1)} %get-tuple-element, ...), custom_call_target="tpu_custom_call" | custom-call | tf_op jit(solution)/shard_map/pallas_call | solution.py:392

commit v6 on v5

--- a/solution.py
+++ b/solution.py
@@ -249,7 +249,7 @@
             pieces.start(*given)
 
         for step in range(steps):
-            c = t - 1 - step
+            c = t - 2 - step
 
             @pl.when((c >= 0) & (c < chunks))
             def _():
@@ -274,7 +274,7 @@
 
         return carry
 
-    lax.fori_loop(0, chunks + steps, tick, 0)
+    lax.fori_loop(0, chunks + steps + 1, tick, 0)
     small_out[...] = little_whole[...]
 
     @pl.when(section == 0)
@@ -395,11 +395,11 @@
         in_specs=[any_space, in_vmem, any_space],
         out_specs=tuple(any_space if n in large else in_vmem for n in range(15)),
         scratch_shapes=[
-            pltpu.VMEM((3, WIDE, WIDE), BF16),
-            pltpu.VMEM((3, WIDE, WIDE), F32),
+            pltpu.VMEM((6, WIDE, WIDE), BF16),
+            pltpu.VMEM((6, WIDE, WIDE), F32),
             pltpu.VMEM(ends.shape, BF16),
-            pltpu.SemaphoreType.DMA((3,)),
-            pltpu.SemaphoreType.DMA((3,)),
+            pltpu.SemaphoreType.DMA((6,)),
+            pltpu.SemaphoreType.DMA((6,)),
             pltpu.SemaphoreType.DMA((2,)),
         ],
         compiler_params=pltpu.CompilerParams(vmem_limit_bytes=60 * 1024 * 1024),

time: 390 us -> 387 us (level)
  no operation moved by 1% of the time
where the time goes in v6:
time: 387 us
  Pallas kernels  384 us (99%)
    pallas_call x1, Pallas kernels, layers(): pl.pallas_call(functools.partial(layers_kernel, mesh.shape['ctx']), out_s...  192 us
    pallas_call x1, Pallas kernels, reduced(): pl.pallas_call(functools.partial(reduce_kernel, orders, mesh.shape['ctx']...  176 us
    pallas_call x1, Pallas kernels, finished(): pl.pallas_call(finish_kernel, out_shape=tuple(shapes), in_specs=[any_spac...  16.6 us

profile of v6, /device:TPU:0, one launch (start us, length us, event | category | flops | bytes accessed | tf_op | source)
XLA Modules:
  0.0 387.2 jit_solution(3443365406280903563)
XLA Ops:
  0.6 0.8 copy.32
  1.4 0.8 copy.33
  2.2 0.7 pad_add_fusion.refs_1_
  2.8 192.0 %shard_map.280 = (bf16[16,768,768]{2,1,0:T(8,128)(2,1)}, bf16[768,768]{1,0:T(8,128)(2,1)}, f32[256,768]{1,0:T(8,128)}) custom-call(bf16[1,6,128,768]{3,2,1,0:T(8,128)(2,1)} %refs_0_.1, s32[6,4]{1,0:T(8,128)} %pad_add_fusion.refs_1_, bf16[1,768]{1,0:T(2,128)(2,1)} %refs_2_.1, bf16[1,768]{1,0:T(2,128)(2,1)} %refs_3_.1, bf16[1,768,2304]{2,1,0:T(8,128)(2,1)} %refs_4_.1, ...), custom_call_target="tpu_custom_call" | custom-call | tf_op jit(solution)/shard_map/pallas_call | solution.py:968
  194.8 175.6 %shard_map.281 = (bf16[12,768,768]{2,1,0:T(8,128)(2,1)}, bf16[256,768]{1,0:T(8,128)(2,1)}, bf16[6,128,768]{2,1,0:T(8,128)(2,1)}) custom-call(bf16[16,768,768]{2,1,0:T(8,128)(2,1)} %get-tuple-element.21.x_ref, f32[256,768]{1,0:T(8,128)} %get-tuple-element.22.small_ref, bf16[768,768]{1,0:T(8,128)(2,1)} %get-tuple-element.23.ends), custom_call_target="tpu_custom_call" | custom-call | tf_op jit(solution)/shard_map/pallas_call | solution.py:302
  370.5 16.6 %shard_map.282 = (bf16[1,6,128,768]{3,2,1,0:T(8,128)(2,1)}, f32[1,768]{1,0:T(1,128)}, f32[1,768]{1,0:T(1,128)}, f32[1,768,2304]{2,1,0:T(8,128)}, f32[1,2304]{1,0...) custom-call(bf16[12,768,768]{2,1,0:T(8,128)(2,1)} %get-tuple-element, ...), custom_call_target="tpu_custom_call" | custom-call | tf_op jit(solution)/shard_map/pallas_call | solution.py:392
